TPU v7x, 256 devices: a whole 4x4x8 slice. The times are simulated.
256 devices in a mesh: rad: 16 (over x_lo, y, core), mode: 16 (over x_hi, z).
Axes of the slice: x: 4 (x_hi: 2, x_lo: 2; x = x_hi * 2 + x_lo), y: 4, z: 8, core: 2. Of those that a mesh axis runs over, the one named last changes fastest.
Arguments:
- field_state: float32 [2, 640, 262144], P(None, 'rad', 'mode'), may hold values from -6 to 6
- forcing: bfloat16 [2, 640, 262144], P(None, 'rad', 'mode'), may hold values from -6 to 6
- inverses: bfloat16 [2, 256, 640, 640], P(None, ('rad', 'mode')), may hold values from -1 to 2
- owned_degree: int32 [256], P(('rad', 'mode')), may hold values from 0 to 767
Outputs:
- section_fields: bfloat16 [2, 640, 262144], P(None, 'rad', 'mode')
All inputs are finite; a program needn't handle non-finite values.
Results may differ from a plain program's by a relative error of at most 0.0049.
Values may be sent and summed in bfloat16 or wider, within the bound.
No kernel may reach another device: no remote copies, remote signals or barrier semaphores. Data moves between devices by JAX's collectives and lax.ppermute only.
A program may use at most 128 MiB of HBM per device.

v0:
```python
import jax
import jax.numpy as jnp
from jax import lax
from jax.sharding import PartitionSpec as P

R_INNER = 0.35
R_OUTER = 1.0
EXPLICIT_WEIGHT = (0.45, 0.35)
FORCING_STEP = 0.5


def explicit_update(values, forcing, below, above, radius_grid, degree_term, spacing):
    weights = jnp.array(EXPLICIT_WEIGHT, jnp.float32)[:, None, None]
    ratio = (spacing / radius_grid)[None, :, None]
    second = above - 2.0 * values + below
    slope = ratio * (above - below)
    horizontal = (
        spacing
        * spacing
        * degree_term[None, None, :]
        / (radius_grid * radius_grid)[None, :, None]
        * values
    )
    return (
        values
        + FORCING_STEP * forcing.astype(jnp.float32)
        + weights * (second + slope - horizontal)
    )


def body(field_state, forcing, inverses, owned_degree):
    row_count = field_state.shape[1]
    group_cols = field_state.shape[2]
    rad_count = lax.axis_size("rad")
    whole_rows = row_count * rad_count
    dev_cols = group_cols // rad_count
    spacing = (R_OUTER - R_INNER) / (whole_rows - 1)
    state_view = field_state.reshape(2, row_count, rad_count, dev_cols)
    state_all = lax.all_to_all(
        lax.all_to_all(state_view, "rad", split_axis=2, concat_axis=1, tiled=True),
        "mode",
        split_axis=3,
        concat_axis=3,
        tiled=True,
    ).reshape(2, whole_rows, dev_cols)
    forcing_view = forcing.reshape(2, row_count, rad_count, dev_cols)
    forcing_all = lax.all_to_all(
        lax.all_to_all(forcing_view, "rad", split_axis=2, concat_axis=1, tiled=True),
        "mode",
        split_axis=3,
        concat_axis=3,
        tiled=True,
    ).reshape(2, whole_rows, dev_cols)
    radius_grid = R_INNER + spacing * jnp.arange(whole_rows, dtype=jnp.int32).astype(jnp.float32)
    degree = owned_degree.astype(jnp.float32)
    degree_term = degree * (degree + 1.0)
    zero_row = jnp.zeros((2, 1, dev_cols), jnp.float32)
    below = jnp.concatenate([zero_row, state_all[:, :-1]], axis=1)
    above = jnp.concatenate([state_all[:, 1:], zero_row], axis=1)
    regrouped = explicit_update(
        state_all, forcing_all, below, above, radius_grid, degree_term, spacing
    ).astype(jnp.bfloat16)
    solved = jnp.einsum(
        "fij,fjc->fic", inverses[:, 0], regrouped, preferred_element_type=jnp.float32
    ).astype(jnp.bfloat16)
    returned = lax.all_to_all(
        lax.all_to_all(
            solved.reshape(2, whole_rows, 1, dev_cols),
            "rad",
            split_axis=1,
            concat_axis=2,
            tiled=True,
        ),
        "mode",
        split_axis=3,
        concat_axis=3,
        tiled=True,
    )
    return returned.reshape(2, row_count, group_cols)


def solution(mesh):
    in_specs = (
        P(None, "rad", "mode"),
        P(None, "rad", "mode"),
        P(None, ("rad", "mode"), None, None),
        P(("rad", "mode")),
    )
    out_specs = P(None, "rad", "mode")
    return jax.shard_map(body, mesh=mesh, in_specs=in_specs, out_specs=out_specs, check_vma=False)
```

profile of v0, /device:TPU:1, one launch (start us, length us, event | category | flops | bytes accessed | tf_op | source)
XLA Modules:
  0.0 541.0 jit_solution(16913794007473105838)
XLA Ops:
  0.0 0.0 copy-start
  0.0 3.7 copy.47
  3.7 7.4 %all-to-all-start.2 = ((bf16[2,40,16,1024]{3,1,0,2:T(8,128)(2,1)}), bf16[2,40,16,1024]{3,1,0,2:T(8,128)(2,1)}, u32[]{:S(2)}, u32[]{:S(2)}) async-start(bf16[2,40,16,1024]{3,1,0,2:T(8,128)(2,1)} %bitcast.54), calls=%async_computation.2 | async-start | bytes 5242880 | tf_op jit(solution)/shard_map/all_to_all | solution.py:48
  11.1 5.7 %copy.46 = f32[2,5,16,8,1024]{4,3,1,0,2:T(8,128)} copy(f32[2,5,16,8,1024]{4,3,2,1,0:T(8,128)} %bitcast.57) | data formatting | bytes 10485760 | tf_op jit(solution)/shard_map/reshape | solution.py:38
  16.8 28.2 %all-to-all-done.2 = bf16[2,40,16,1024]{3,1,0,2:T(8,128)(2,1)} async-done(((bf16[2,40,16,1024]{3,1,0,2:T(8,128)(2,1)}), bf16[2,40,16,1024]{3,1,0,2:T(8,128)(2,1)}, u32[]{:S(2)}, u32[]{:S(2)}) %all-to-all-start.2) | async-done | bytes 2621472 | tf_op jit(solution)/shard_map/all_to_all | solution.py:48
  45.0 8.5 %all-to-all-start = ((f32[2,40,16,1024]{3,1,0,2:T(8,128)}), f32[2,40,16,1024]{3,1,0,2:T(8,128)}, u32[]{:S(2)}, u32[]{:S(2)}) async-start(f32[2,40,16,1024]{3,1,0,2:T(8,128)} %bitcast.52), calls=%async_computation | async-start | bytes 10485760 | tf_op jit(solution)/shard_map/all_to_all | solution.py:40
  53.5 3.5 copy.33
  57.0 7.5 %copy.34 = bf16[2,640,1,1024]{1,0,2,3:T(2,128)(2,1)} copy(bf16[2,640,1,1024]{3,1,0,2:T(8,128)(2,1)} %bitcast.55) | data formatting | bytes 5242880 | tf_op jit(solution)/shard_map/all_to_all | solution.py:48
  64.5 60.7 %all-to-all-done = f32[2,40,16,1024]{3,1,0,2:T(8,128)} async-done(((f32[2,40,16,1024]{3,1,0,2:T(8,128)}), f32[2,40,16,1024]{3,1,0,2:T(8,128)}, u32[]{:S(2)}, u32[]{:S(2)}) %all-to-all-start) | async-done | bytes 5242912 | tf_op jit(solution)/shard_map/all_to_all | solution.py:40
  125.2 10.2 %all-to-all-start.3 = ((bf16[2,640,1,1024]{1,0,2,3:T(2,128)(2,1)}), bf16[2,640,1,1024]{1,0,2,3:T(2,128)(2,1)}, u32[]{:S(2)}, u32[]{:S(2)}) async-start(bf16[2,640,1,1024]{1,0,2,3:T(2,128)(2,1)} %copy.34), calls=%async_computation.3 | async-start | bytes 5242880 | tf_op jit(solution)/shard_map/all_to_all | solution.py:47
  135.5 5.7 %copy.29 = f32[2,40,16,1024]{3,1,2,0:T(8,128)} copy(f32[2,40,16,1024]{3,1,0,2:T(8,128)} %all-to-all-done) | data formatting | bytes 10485760 | tf_op jit(solution)/shard_map/all_to_all | solution.py:40
  141.2 8.8 %copy.30 = f32[2,640,1,1024]{1,0,2,3:T(2,128)} copy(f32[2,640,1,1024]{3,1,0,2:T(8,128)} %bitcast.53) | data formatting | bytes 10485760 | tf_op jit(solution)/shard_map/all_to_all | solution.py:40
  150.0 48.0 %all-to-all-done.3 = bf16[2,640,1,1024]{1,0,2,3:T(2,128)(2,1)} async-done(((bf16[2,640,1,1024]{1,0,2,3:T(2,128)(2,1)}), bf16[2,640,1,1024]{1,0,2,3:T(2,128)(2,1)}, u32[]{:S(2)}, u32[]{:S(2)}) %all-to-all-start.3) | async-done | bytes 2621472 | tf_op jit(solution)/shard_map/all_to_all | solution.py:47
  198.0 7.5 %all-to-all-start.1 = ((f32[2,640,1,1024]{1,0,2,3:T(2,128)}), f32[2,640,1,1024]{1,0,2,3:T(2,128)}, u32[]{:S(2)}, u32[]{:S(2)}) async-start(f32[2,640,1,1024]{1,0,2,3:T(2,128)} %copy.30), calls=%async_computation.1 | async-start | bytes 10485760 | tf_op jit(solution)/shard_map/all_to_all | solution.py:39
  206.2 7.4 %copy.35 = bf16[2,640,1,1024]{3,1,2,0:T(8,128)(2,1)} copy(bf16[2,640,1,1024]{1,0,2,3:T(2,128)(2,1)} %all-to-all-done.3) | data formatting | bytes 5242880 | tf_op jit(solution)/shard_map/all_to_all | solution.py:47
  213.6 110.7 %all-to-all-done.1 = f32[2,640,1,1024]{1,0,2,3:T(2,128)} async-done(((f32[2,640,1,1024]{1,0,2,3:T(2,128)}), f32[2,640,1,1024]{1,0,2,3:T(2,128)}, u32[]{:S(2)}, u32[]{:S(2)}) %all-to-all-start.1) | async-done | bytes 5242912 | tf_op jit(solution)/shard_map/all_to_all | solution.py:39
  324.2 8.7 %copy.31 = f32[2,640,1,1024]{3,1,0,2:T(8,128)} copy(f32[2,640,1,1024]{1,0,2,3:T(2,128)} %all-to-all-done.1) | data formatting | bytes 10485760 | tf_op jit(solution)/shard_map/all_to_all | solution.py:39
  332.9 0.0 copy-start.2
  332.9 10.4 %fusion.12 = (f32[2,639,1024]{2,1,0:T(8,128)}, f32[2,639,1024]{2,1,0:T(8,128)}) fusion(f32[2,640,1024]{2,1,0:T(8,128)} %bitcast.49), kind=kLoop, calls=%fused_computation.15 | loop fusion | bytes 20938752 | tf_op jit(solution)/shard_map/slice | solution.py:59
  343.4 0.0 copy-done
  343.4 0.0 copy-done.2
  343.4 12.5 %convert_bitcast_fusion = bf16[2,640,1,1024]{1,3,0,2:T(8,128)(2,1)} fusion(f32[2,639,1024]{2,1,0:T(8,128)} %get-tuple-element.6, f32[2,639,1024]{2,1,0:T(8,128)} %get-tuple-element.5, bf16[2,640,1,1024]{3,1,2,0:T(8,128)(2,1)} %copy.35, f32[640]{0:T(1024)S(1)} %get-tuple-element.7, f32[640]{0:T(1024)S(1)} %get-tuple-element.8, f32[2]{0:T(128)S(1)} %copy-done.2, ...), kind=kOutput, calls=%fused_computation.5 | convolution fusion | flops 1697382400 | bytes 22598664 | tf_op jit(solution)/shard_map/fij,fjc->fic/dot_general | solution.py:63
  355.9 7.5 %copy.37 = bf16[2,640,1,1024]{3,0,2,1:T(2,128)(2,1)} copy(bf16[2,640,1,1024]{1,3,0,2:T(8,128)(2,1)} %convert_bitcast_fusion) | data formatting | bytes 5242880 | tf_op jit(solution)/shard_map/reshape | solution.py:68
  363.4 44.7 %all_to_all.69 = bf16[2,640,1,1024]{3,0,2,1:T(2,128)(2,1)S(1)} all-to-all(bf16[2,640,1,1024]{3,0,2,1:T(2,128)(2,1)} %copy.37), channel_id=1, replica_groups=mesh['rad'=16,'mode'=16] {'rad'}, dimensions={1} | all-to-all | bytes 5242880 | tf_op jit(solution)/shard_map/all_to_all | solution.py:67
  408.1 2.3 copy.38
  410.4 12.6 %copy.39 = bf16[2,40,16,1024]{1,2,0,3:T(8,128)(2,1)} copy(bf16[2,40,16,1024]{3,1,2,0:T(8,128)(2,1)} %bitcast.56) | data formatting | bytes 5242880 | tf_op jit(solution)/shard_map/all_to_all | solution.py:67
  423.1 16.6 %reshape.42 = bf16[16,2,40960]{2,1,0:T(2,128)(2,1)} reshape(bf16[1024,2,16,40]{3,2,1,0:T(8,128)(2,1)} %bitcast.50) | data formatting | bytes 5242880
  439.7 68.0 %all_to_all.70 = bf16[16,2,40960]{2,1,0:T(2,128)(2,1)} all-to-all(bf16[16,2,40960]{2,1,0:T(2,128)(2,1)} %reshape.42), channel_id=1, replica_groups=mesh['rad'=16,'mode'=16] {'mode'}, dimensions={0} | all-to-all | bytes 5242880 | tf_op jit(solution)/shard_map/all_to_all | solution.py:66
  507.6 16.9 %reshape.43 = bf16[1024,2,16,40]{3,2,1,0:T(8,128)(2,1)} reshape(bf16[16,2,40960]{2,1,0:T(2,128)(2,1)} %all_to_all.70) | data formatting | bytes 5242880
  524.5 0.0 copy-start.1
  524.5 11.2 %copy.40 = bf16[2,40,16,1024]{3,2,1,0:T(8,128)(2,1)} copy(bf16[2,40,16,1024]{1,2,0,3:T(8,128)(2,1)} %bitcast.51) | data formatting | bytes 5242880 | tf_op jit(solution)/shard_map/all_to_all | solution.py:66
  535.8 5.3 reshape.41
  541.0 0.0 copy-done.1
  (1 shorter events, 0.0 us)
Async XLA Ops:
  0.0 343.4 %copy-start = (bf16[2,1,640,640]{3,2,1,0:T(8,128)(2,1)S(1)}, bf16[2,1,640,640]{3,2,1,0:T(8,128)(2,1)}, u32[]{:S(2)}) copy-start(bf16[2,1,640,640]{3,2,1,0:T(8,128)(2,1)} %param.7) | copy-start | bytes 4915204
  3.7 41.3 %all-to-all-start.2 = ((bf16[2,40,16,1024]{3,1,0,2:T(8,128)(2,1)}), bf16[2,40,16,1024]{3,1,0,2:T(8,128)(2,1)}, u32[]{:S(2)}, u32[]{:S(2)}) async-start(bf16[2,40,16,1024]{3,1,0,2:T(8,128)(2,1)} %bitcast.54), calls=%async_computation.2 | async-start | bytes 5242880 | tf_op jit(solution)/shard_map/all_to_all | solution.py:48
  45.0 80.2 %all-to-all-start = ((f32[2,40,16,1024]{3,1,0,2:T(8,128)}), f32[2,40,16,1024]{3,1,0,2:T(8,128)}, u32[]{:S(2)}, u32[]{:S(2)}) async-start(f32[2,40,16,1024]{3,1,0,2:T(8,128)} %bitcast.52), calls=%async_computation | async-start | bytes 10485760 | tf_op jit(solution)/shard_map/all_to_all | solution.py:40
  125.2 72.8 %all-to-all-start.3 = ((bf16[2,640,1,1024]{1,0,2,3:T(2,128)(2,1)}), bf16[2,640,1,1024]{1,0,2,3:T(2,128)(2,1)}, u32[]{:S(2)}, u32[]{:S(2)}) async-start(bf16[2,640,1,1024]{1,0,2,3:T(2,128)(2,1)} %copy.34), calls=%async_computation.3 | async-start | bytes 5242880 | tf_op jit(solution)/shard_map/all_to_all | solution.py:47
  198.0 126.2 %all-to-all-start.1 = ((f32[2,640,1,1024]{1,0,2,3:T(2,128)}), f32[2,640,1,1024]{1,0,2,3:T(2,128)}, u32[]{:S(2)}, u32[]{:S(2)}) async-start(f32[2,640,1,1024]{1,0,2,3:T(2,128)} %copy.30), calls=%async_computation.1 | async-start | bytes 10485760 | tf_op jit(solution)/shard_map/all_to_all | solution.py:39
  332.9 10.4 %copy-start.2 = (f32[2]{0:T(128)S(1)}, f32[2]{0:T(128)}, u32[]{:S(2)}) copy-start(f32[2]{0:T(128)} %constant.17.clone) | copy-start | bytes 28
  524.5 16.5 %copy-start.1 = (bf16[2,1,640,640]{3,2,1,0:T(8,128)(2,1)S(1)}, bf16[2,1,640,640]{3,2,1,0:T(8,128)(2,1)}, u32[]{:S(2)}) copy-start(bf16[2,1,640,640]{3,2,1,0:T(8,128)(2,1)} %param.7) | copy-start | bytes 4915204
where the time goes:
time: 545 us; the launch traced here: 541 us
  waiting for transfers between devices  248 us (46%)
  local copies, waits for them, and re-layouts  134 us (25%)
  blocking collectives  113 us (21%)
  starting transfers between devices  33.7 us (6%)
  matrix products  12.5 us (2%)
    all_to_all x1, waiting for transfers between devices, body(): lax.all_to_all(lax.all_to_all(state_view, 'rad', split_axis=2, concat_axi...  111 us
    all_to_all x1, blocking collectives, body(): lax.all_to_all(lax.all_to_all(solved.reshape(2, whole_rows, 1, dev_cols),...  68 us
    all_to_all x1, waiting for transfers between devices, body(): lax.all_to_all(state_view, 'rad', split_axis=2, concat_axis=1, tiled=True)  60.7 us
    all_to_all x1, waiting for transfers between devices, body(): lax.all_to_all(lax.all_to_all(forcing_view, 'rad', split_axis=2, concat_a...  48 us
    all_to_all x1, blocking collectives, body(): lax.all_to_all(solved.reshape(2, whole_rows, 1, dev_cols), 'rad', split_a...  44.7 us
    unnamed x8, local copies, waits for them, and re-layouts  33.5 us
    all_to_all x1, waiting for transfers between devices, body(): lax.all_to_all(forcing_view, 'rad', split_axis=2, concat_axis=1, tiled=True)  28.2 us
    all_to_all x2, local copies, waits for them, and re-layouts, body(): lax.all_to_all(solved.reshape(2, whole_rows, 1, dev_cols), 'rad', split_a...  14.9 us
  transfers between devices with their start and end apart: 4, of which 4 were waited for; matrix products, arithmetic and copies ran while one was open for 7% of the time, Pallas kernels for 0%

commit v1 on v0

v1 whole, which is shorter than its diff:
```python
import functools

import jax
import jax.numpy as jnp
from jax import lax
from jax.experimental import pallas as pl
from jax.experimental.pallas import tpu as pltpu
from jax.sharding import PartitionSpec as P

R_INNER = 0.35
R_OUTER = 1.0
EXPLICIT_WEIGHT = (0.45, 0.35)
FORCING_STEP = 0.5
AXES = ("rad", "mode")
LANES = 128


def pair_lanes(first, second, low):
    mixed = pltpu.roll(jnp.where(low, second, first), LANES // 2, axis=1)
    return jnp.where(low, first, mixed), jnp.where(low, mixed, second)


def right_side_kernel(spacing, piece, degree_ref, up_ref, down_ref, state_ref, forcing_ref, out_ref):
    rows, cols = state_ref.shape[1:]
    start = pl.program_id(0) * (cols // piece)
    row = lax.broadcasted_iota(jnp.int32, (rows, LANES), 0)
    low = lax.broadcasted_iota(jnp.int32, (rows, LANES), 1) < piece
    first_row, last_row = row == 0, row == rows - 1
    radius = R_INNER + spacing * (lax.axis_index("rad") * rows + row).astype(jnp.float32)
    ratio = spacing / radius
    square = (spacing * spacing) / (radius * radius)
    for j in range(cols // LANES):
        lanes = slice(j * LANES, (j + 1) * LANES)
        even = degree_ref[start + 2 * j]
        odd = degree_ref[start + 2 * j + 1]
        degree_term = jnp.where(low, even * (even + 1.0), odd * (odd + 1.0))
        horizontal = square * degree_term
        sides = []
        for f, weight in enumerate(EXPLICIT_WEIGHT):
            values = state_ref[f, :, lanes]
            above = jnp.where(last_row, up_ref[f, :, lanes], pltpu.roll(values, rows - 1, axis=0))
            below = jnp.where(first_row, down_ref[f, :, lanes], pltpu.roll(values, 1, axis=0))
            sides.append(
                values
                + FORCING_STEP * forcing_ref[f, :, lanes].astype(jnp.float32)
                + weight
                * ((above - 2.0 * values + below) + ratio * (above - below) - horizontal * values)
            )
        first, second = pair_lanes(sides[0], sides[1], low)
        out_ref[2 * j] = first.astype(jnp.bfloat16)
        out_ref[2 * j + 1] = second.astype(jnp.bfloat16)


def solve_kernel(piece, inverse_ref, side_ref, out_ref):
    senders, groups, rows, _ = side_ref.shape
    whole = senders * rows
    sides = [
        side_ref[:, g].astype(jnp.float32).reshape(whole, LANES).astype(jnp.bfloat16)
        for g in range(groups)
    ]
    side = jnp.concatenate(sides, axis=1)
    low = lax.broadcasted_iota(jnp.int32, (whole, groups * LANES), 1) % LANES < piece
    solved = jnp.where(
        low,
        jnp.dot(inverse_ref[0, 0], side, preferred_element_type=jnp.float32),
        jnp.dot(inverse_ref[1, 0], side, preferred_element_type=jnp.float32),
    )
    for g in range(groups):
        out_ref[:, g] = (
            solved[:, g * LANES : (g + 1) * LANES]
            .reshape(senders, rows, LANES)
            .astype(jnp.bfloat16)
        )


def unpack_kernel(piece, solved_ref, out_ref):
    owners, rows, _ = solved_ref.shape
    low = lax.broadcasted_iota(jnp.int32, (rows, LANES), 1) < piece
    for j in range(owners // 2):
        lanes = slice(j * LANES, (j + 1) * LANES)
        first, second = pair_lanes(
            solved_ref[2 * j].astype(jnp.float32), solved_ref[2 * j + 1].astype(jnp.float32), low
        )
        out_ref[0, :, lanes] = first.astype(jnp.bfloat16)
        out_ref[1, :, lanes] = second.astype(jnp.bfloat16)


def body(field_state, forcing, inverses, owned_degree):
    fields, rows, group_cols = field_state.shape
    rad_count = lax.axis_size("rad")
    mode_count = lax.axis_size("mode")
    slots = rad_count * mode_count
    whole_rows = rows * rad_count
    piece = group_cols // slots
    spacing = (R_OUTER - R_INNER) / (whole_rows - 1)

    degrees = lax.all_to_all(
        jnp.broadcast_to(owned_degree.astype(jnp.float32), (slots,)), AXES, 0, 0, tiled=True
    )
    from_above = lax.ppermute(
        field_state[:, :1], "rad", [(i + 1, i) for i in range(rad_count - 1)]
    )
    from_below = lax.ppermute(
        field_state[:, rows - 1 :], "rad", [(i, i + 1) for i in range(rad_count - 1)]
    )

    cols = 2048
    packed = pl.pallas_call(
        functools.partial(right_side_kernel, spacing, piece),
        grid=(group_cols // cols,),
        in_specs=[
            pl.BlockSpec(memory_space=pltpu.SMEM),
            pl.BlockSpec((fields, 1, cols), lambda i: (0, 0, i)),
            pl.BlockSpec((fields, 1, cols), lambda i: (0, 0, i)),
            pl.BlockSpec((fields, rows, cols), lambda i: (0, 0, i)),
            pl.BlockSpec((fields, rows, cols), lambda i: (0, 0, i)),
        ],
        out_specs=pl.BlockSpec((cols // piece, rows, LANES), lambda i: (i, 0, 0)),
        out_shape=jax.ShapeDtypeStruct((slots, rows, LANES), jnp.bfloat16),
        name="right_side",
    )(degrees, from_above, from_below, field_state, forcing)

    packed = lax.all_to_all(packed, AXES, 0, 0, tiled=True)

    groups = 4
    solved = pl.pallas_call(
        functools.partial(solve_kernel, piece),
        grid=(mode_count // groups,),
        in_specs=[
            pl.BlockSpec((fields, 1, whole_rows, whole_rows), lambda i: (0, 0, 0, 0)),
            pl.BlockSpec((rad_count, groups, rows, LANES), lambda i: (0, i, 0, 0)),
        ],
        out_specs=pl.BlockSpec((rad_count, groups, rows, LANES), lambda i: (0, i, 0, 0)),
        out_shape=jax.ShapeDtypeStruct((rad_count, mode_count, rows, LANES), jnp.bfloat16),
        compiler_params=pltpu.CompilerParams(vmem_limit_bytes=48 * 1024 * 1024),
        name="solve",
    )(inverses, packed.reshape(rad_count, mode_count, rows, LANES))

    solved = lax.all_to_all(solved.reshape(slots, rows, LANES), AXES, 0, 0, tiled=True)

    owners = 32
    return pl.pallas_call(
        functools.partial(unpack_kernel, piece),
        grid=(slots // owners,),
        in_specs=[pl.BlockSpec((owners, rows, LANES), lambda i: (i, 0, 0))],
        out_specs=pl.BlockSpec((fields, rows, owners * piece), lambda i: (0, 0, i)),
        out_shape=jax.ShapeDtypeStruct((fields, rows, group_cols), jnp.bfloat16),
        name="unpack",
    )(solved)


def solution(mesh):
    in_specs = (
        P(None, "rad", "mode"),
        P(None, "rad", "mode"),
        P(None, ("rad", "mode"), None, None),
        P(("rad", "mode")),
    )
    out_specs = P(None, "rad", "mode")
    return jax.shard_map(body, mesh=mesh, in_specs=in_specs, out_specs=out_specs, check_vma=False)
```

time: 545 us -> 203 us (0.37)
  waiting for transfers between devices: 248 us -> 0.01 us
  local copies, waits for them, and re-layouts: 134 us -> 3.07 us
  blocking collectives: 113 us -> 170 us
  starting transfers between devices: 33.7 us -> 6.52 us
  Pallas kernels: 0 us -> 21.4 us
  matrix products: 12.5 us -> 0 us
    all_to_all x4 -> x0, waiting for transfers between devices: 248 us -> none  [the longest x1 111 us: body(): lax.all_to_all(lax.all_to_all(state_view, 'rad', split_axis=2, concat_axi...]
    all_to_all x9 -> x0, local copies, waits for them, and re-layouts: 67.8 us -> none  [the longest x2 14.9 us: body(): lax.all_to_all(solved.reshape(2, whole_rows, 1, dev_cols), 'rad', split_a...]
    all_to_all x2 -> x3, blocking collectives: 113 us -> 170 us  [the longest x1 71.9 us: body(): packed = lax.all_to_all(packed, AXES, 0, 0, tiled=True)]
    all_to_all x4 -> x0, starting transfers between devices: 33.7 us -> none  [the longest x1 10.2 us: body(): lax.all_to_all(lax.all_to_all(forcing_view, 'rad', split_axis=2, concat_a...]
    unnamed x8 -> x6, local copies, waits for them, and re-layouts: 33.5 us -> 1.28 us
    reshape x4 -> x0, local copies, waits for them, and re-layouts: 22.1 us -> none  [the longest x1 7.47 us: body(): solved.reshape(2, whole_rows, 1, dev_cols)]
    pallas_call x0 -> x3, Pallas kernels: none -> 21.4 us  [the longest x1 8.93 us: body(): pl.pallas_call(functools.partial(right_side_kernel, spacing, piece), grid...]
    dot_general x1 -> x0, matrix products: 12.5 us -> none  [body(): jnp.einsum('fij,fjc->fic', inverses[:, 0], regrouped, preferred_element_t...]
  transfers between devices with their start and end apart: 4 -> 2, of which waited for: 4 -> 0; matrix products, arithmetic and copies ran while one was open for 7% -> 1% of each run, Pallas kernels for 0% -> 0%
where the time goes in v1:
time: 203 us
  blocking collectives  170 us (84%)
  Pallas kernels  21.4 us (11%)
  starting transfers between devices  6.52 us (3%)
  local copies, waits for them, and re-layouts  3.07 us (2%)
    all_to_all x1, blocking collectives, body(): packed = lax.all_to_all(packed, AXES, 0, 0, tiled=True)  71.9 us
    all_to_all x1, blocking collectives, body(): lax.all_to_all(solved.reshape(slots, rows, LANES), AXES, 0, 0, tiled=True)  70.5 us
    all_to_all x1, blocking collectives, body(): lax.all_to_all(jnp.broadcast_to(owned_degree.astype(jnp.float32), (slots,...  27.2 us
    pallas_call x1, Pallas kernels, body(): pl.pallas_call(functools.partial(right_side_kernel, spacing, piece), grid...  8.93 us
    pallas_call x1, Pallas kernels, body(): pl.pallas_call(functools.partial(unpack_kernel, piece), grid=(slots // ow...  6.35 us
    pallas_call x1, Pallas kernels, body(): pl.pallas_call(functools.partial(solve_kernel, piece), grid=(mode_count /...  6.07 us
    ppermute x1, starting transfers between devices, body(): lax.ppermute(field_state[:, rows - 1:], 'rad', [(i, i + 1) for i in range...  4.59 us
  transfers between devices with their start and end apart: 2, of which 0 were waited for; matrix products, arithmetic and copies ran while one was open for 1% of the time, Pallas kernels for 0%

profile of v1, /device:TPU:1, one launch (start us, length us, event | category | flops | bytes accessed | tf_op | source)
XLA Modules:
  0.0 202.9 jit_solution(3003334285878603119)
XLA Ops:
  0.0 1.7 fusion
  1.7 4.6 %collective-permute-start.1 = (f32[2,1,16384]{2,1,0:T(1,128)S(1)}, f32[2,1,16384]{2,1,0:T(1,128)S(1)}, u32[]{:S(2)}, u32[]{:S(2)}) collective-permute-start(f32[2,1,16384]{2,1,0:T(1,128)S(1)} %get-tuple-element.5), channel_id=1, source_target_pairs={{0,16},{16,32},{32,48},{48,64},{64,80},{80,96},{96,112},{112,128},... | collective-permute-start | bytes 393224 | tf_op jit(solution)/shard_map/ppermute | solution.py:103
  6.3 1.9 collective-permute-start
  8.9 0.1 broadcast_in_dim.8
  9.0 27.2 %all_to_all.18 = f32[256,1,1]{2,1,0:T(1,128)S(1)} all-to-all(f32[256,1,1]{2,1,0:T(1,128)S(1)} %broadcast_in_dim.8), channel_id=1, replica_groups=mesh['rad'=16,'mode'=16] {'rad','mode'}, dimensions={0} | all-to-all | bytes 2048 | tf_op jit(solution)/shard_map/all_to_all | solution.py:97
  36.2 1.6 reduce.degree_ref
  37.8 0.0 collective-permute-done.1.down_ref
  37.8 0.0 copy-start.1
  37.8 0.0 collective-permute-done.up_ref
  37.8 0.6 copy-done.1
  38.4 0.0 copy-start.2
  38.4 0.6 copy-done.2
  39.1 8.9 %right_side.1 = bf16[256,40,128]{2,1,0:T(8,128)(2,1)} custom-call(f32[256]{0:T(256)} %reduce.degree_ref, f32[2,1,16384]{2,1,0:T(1,128)} %copy-done.2, f32[2,1,16384]{2,1,0:T(1,128)} %copy-done.1, f32[2,40,16384]{2,1,0:T(8,128)} %state_ref.1, bf16[2,40,16384]{2,1,0:T(8,128)(2,1)} %forcing_ref.1), custom_call_target="tpu_custom_call" | custom-call | tf_op jit(solution)/shard_map/right_side/pallas_call | solution.py:108
  48.0 0.0 copy-start
  48.0 71.9 %all_to_all.19 = bf16[256,40,128]{2,1,0:T(8,128)(2,1)} all-to-all(bf16[256,40,128]{2,1,0:T(8,128)(2,1)} %right_side.1), channel_id=1, replica_groups=mesh['rad'=16,'mode'=16] {'rad','mode'}, dimensions={0} | all-to-all | bytes 5242880 | tf_op jit(solution)/shard_map/all_to_all | solution.py:123
  119.9 0.0 copy-done
  119.9 6.1 %solve.1 = bf16[16,16,40,128]{3,2,1,0:T(8,128)(2,1)S(1)} custom-call(bf16[2,1,640,640]{3,2,1,0:T(8,128)(2,1)S(1)} %copy-done, bf16[16,16,40,128]{3,2,1,0:T(8,128)(2,1)} %bitcast.4), custom_call_target="tpu_custom_call" | custom-call | tf_op jit(solution)/shard_map/solve/pallas_call | solution.py:126
  126.0 70.5 %all_to_all.20.solved_ref = bf16[256,40,128]{2,1,0:T(8,128)(2,1)} all-to-all(bf16[256,40,128]{2,1,0:T(8,128)(2,1)S(1)} %bitcast.3), channel_id=1, replica_groups=mesh['rad'=16,'mode'=16] {'rad','mode'}, dimensions={0} | all-to-all | bytes 5242880 | tf_op jit(solution)/shard_map/all_to_all | solution.py:139
  196.5 6.4 %unpack.1 = bf16[2,40,16384]{2,1,0:T(8,128)(2,1)} custom-call(bf16[256,40,128]{2,1,0:T(8,128)(2,1)} %all_to_all.20.solved_ref), custom_call_target="tpu_custom_call" | custom-call | tf_op jit(solution)/shard_map/unpack/pallas_call | solution.py:142
Async XLA Ops:
  1.7 36.0 %collective-permute-start.1 = (f32[2,1,16384]{2,1,0:T(1,128)S(1)}, f32[2,1,16384]{2,1,0:T(1,128)S(1)}, u32[]{:S(2)}, u32[]{:S(2)}) collective-permute-start(f32[2,1,16384]{2,1,0:T(1,128)S(1)} %get-tuple-element.5), channel_id=1, source_target_pairs={{0,16},{16,32},{32,48},{48,64},{64,80},{80,96},{96,112},{112,128},... | collective-permute-start | bytes 393224 | tf_op jit(solution)/shard_map/ppermute | solution.py:103
  6.3 31.4 %collective-permute-start = (f32[2,1,16384]{2,1,0:T(1,128)S(1)}, f32[2,1,16384]{2,1,0:T(1,128)S(1)}, u32[]{:S(2)}, u32[]{:S(2)}) collective-permute-start(f32[2,1,16384]{2,1,0:T(1,128)S(1)} %get-tuple-element.6), channel_id=1, source_target_pairs={{16,0},{32,16},{48,32},{64,48},{80,64},{96,80},{112,96},{128,112},... | collective-permute-start | bytes 393224 | tf_op jit(solution)/shard_map/ppermute | solution.py:100
  37.8 0.6 copy-start.1
  38.4 0.6 copy-start.2
  48.0 71.9 %copy-start = (bf16[2,1,640,640]{3,2,1,0:T(8,128)(2,1)S(1)}, bf16[2,1,640,640]{3,2,1,0:T(8,128)(2,1)}, u32[]{:S(2)}) copy-start(bf16[2,1,640,640]{3,2,1,0:T(8,128)(2,1)} %inverse_ref.1) | copy-start | bytes 4915204

commit v2 on v0

v2 whole, which is shorter than its diff:
```python
import functools

import jax
import jax.numpy as jnp
from jax import lax
from jax.experimental import pallas as pl
from jax.experimental.pallas import tpu as pltpu
from jax.sharding import PartitionSpec as P

R_INNER = 0.35
R_OUTER = 1.0
EXPLICIT_WEIGHT = (0.45, 0.35)
FORCING_STEP = 0.5
AXES = ("rad", "mode")
LANES = 128
CORES = 2
DEPTH = 8
QUAD = DEPTH // 2
SMALL_VMEM = 24 * 1024 * 1024
LARGE_VMEM = 56 * 1024 * 1024


def pair_lanes(first, second, low):
    mixed = pltpu.roll(jnp.where(low, second, first), LANES // 2, axis=1)
    return jnp.where(low, first, mixed), jnp.where(low, mixed, second)


def slot_of(z, core, quad):
    turned = (z + DEPTH - CORES * core) % DEPTH
    inside = turned // QUAD == quad
    at = turned % QUAD
    return jnp.where(inside, at, QUAD - 1 - at), jnp.where(inside, 0, 1)


def right_side_kernel(
    spacing,
    piece,
    place_ref,
    degree_ref,
    same_ref,
    cross_ref,
    own_ref,
    own_forcing_ref,
    other_ref,
    other_forcing_ref,
    out_ref,
    state_buf,
    forcing_buf,
    out_buf,
    radial_buf,
    in_sem,
    out_sem,
):
    core, quad = place_ref[0], place_ref[1]
    chunks, _, fields, rows, cols = state_buf.shape
    whole = CORES * rows
    peers = out_buf.shape[0] // chunks

    def reads(i):
        columns = pl.ds(pl.multiple_of((CORES * i + core) * cols, cols), cols)
        pairs = [
            (own_ref, state_buf, core),
            (own_forcing_ref, forcing_buf, core),
            (other_ref, state_buf, 1 - core),
            (other_forcing_ref, forcing_buf, 1 - core),
        ]
        return [
            pltpu.make_async_copy(source.at[:, :, columns], target.at[i, which], in_sem.at[i, n])
            for n, (source, target, which) in enumerate(pairs)
        ]

    def write(i):
        block = pl.ds(i * peers, peers)
        return pltpu.make_async_copy(out_buf.at[block], out_ref.at[block], out_sem.at[i])

    for i in range(chunks):
        for copy in reads(i):
            copy.start()

    row = lax.broadcasted_iota(jnp.int32, (whole, LANES), 0)
    low = lax.broadcasted_iota(jnp.int32, (whole, LANES), 1) < piece
    first_row, last_row = row[:8] == 0, row[whole - 8 :] == whole - 1
    chip = lax.axis_index("rad") // CORES
    radius = R_INNER + spacing * (chip * whole + row).astype(jnp.float32)
    ratio = spacing / radius
    square = (spacing * spacing) / (radius * radius)
    for f, weight in enumerate(EXPLICIT_WEIGHT):
        radial_buf[f, 0] = weight * (1.0 + ratio)
        radial_buf[f, 1] = weight * (1.0 - ratio)
        radial_buf[f, 2] = weight * square

    @pl.loop(0, chunks)
    def _(i):
        for copy in reads(i):
            copy.wait()
        for j in range(cols // LANES):
            lanes = slice(j * LANES, (j + 1) * LANES)
            columns = pl.ds(
                pl.multiple_of((CORES * i + core) * cols + j * LANES, LANES), LANES
            )
            degree = jnp.where(
                low[:1], degree_ref[i, 2 * j : 2 * j + 1], degree_ref[i, 2 * j + 1 : 2 * j + 2]
            )
            term = degree * (degree + 1.0)
            sides = []
            for f, weight in enumerate(EXPLICIT_WEIGHT):
                same, cross = same_ref[f, :, columns], cross_ref[f, :, columns]
                above_edge = jnp.where(core == 0, same, cross)
                below_edge = jnp.where(core == 0, cross, same)
                values = jnp.concatenate([state_buf[i, c, f, :, lanes] for c in range(CORES)], axis=0)
                extra = jnp.concatenate(
                    [forcing_buf[i, c, f, :, lanes].astype(jnp.float32) for c in range(CORES)], axis=0
                )
                above = pltpu.roll(values, whole - 1, axis=0)
                below = pltpu.roll(values, 1, axis=0)
                above = jnp.concatenate(
                    [above[: whole - 8], jnp.where(last_row, above_edge, above[whole - 8 :])], axis=0
                )
                below = jnp.concatenate(
                    [jnp.where(first_row, below_edge, below[:8]), below[8:]], axis=0
                )
                sides.append(
                    values * ((1.0 - 2.0 * weight) - radial_buf[f, 2] * term)
                    + FORCING_STEP * extra
                    + above * radial_buf[f, 0]
                    + below * radial_buf[f, 1]
                )
            pieces = pair_lanes(*sides, low)
            half, pair = divmod(2 * j, DEPTH)
            for parity in range(2):
                at, slot = slot_of(pair + parity, core, quad)
                out_buf[i * peers + half * QUAD + at, slot] = (
                    pieces[parity].reshape(CORES, rows, LANES).astype(jnp.bfloat16)
                )
        write(i).start()

    for i in range(chunks):
        write(i).wait()


def solve_kernel(piece, own_ref, *refs):
    *mirror_refs, side_ref, out_ref = refs
    chips, groups, slots, cores, rows, _ = side_ref.shape
    whole = chips * cores * rows
    low = lax.broadcasted_iota(jnp.int32, (whole, groups * LANES), 1) % LANES < piece
    own = [own_ref[f, 0] for f in range(own_ref.shape[0])]
    mirror = [ref[0, 0] for ref in mirror_refs]
    for slot, inverse in enumerate((own, mirror)):
        side = jnp.concatenate(
            [
                side_ref[:, g, slot].astype(jnp.float32).reshape(whole, LANES).astype(jnp.bfloat16)
                for g in range(groups)
            ],
            axis=1,
        )
        solved = jnp.where(
            low,
            jnp.dot(inverse[0], side, preferred_element_type=jnp.float32),
            jnp.dot(inverse[1], side, preferred_element_type=jnp.float32),
        )
        for g in range(groups):
            out_ref[:, g, slot] = (
                solved[:, g * LANES : (g + 1) * LANES]
                .reshape(chips, cores, rows, LANES)
                .astype(jnp.bfloat16)
            )


def unpack_kernel(piece, turn, place_ref, solved_ref, *refs):
    out_ref, in_buf, out_buf, in_sem, out_sem = refs[-5:]
    here = place_ref[0]
    core = here if turn == 0 else 1 - here
    quad = place_ref[1 + turn]
    chunks, peers = in_buf.shape[:2]
    rows, cols = out_buf.shape[2:]
    low = lax.broadcasted_iota(jnp.int32, (rows, LANES), 1) < piece

    def read(i):
        return pltpu.make_async_copy(
            solved_ref.at[pl.ds(i * peers, peers), :, here], in_buf.at[i], in_sem.at[i]
        )

    def write(i):
        columns = pl.ds(pl.multiple_of((CORES * i + core) * cols, cols), cols)
        return pltpu.make_async_copy(out_buf.at[i], out_ref.at[:, :, columns], out_sem.at[i])

    for i in range(chunks):
        read(i).start()

    @pl.loop(0, chunks)
    def _(i):
        read(i).wait()
        for j in range(cols // LANES):
            lanes = slice(j * LANES, (j + 1) * LANES)
            half, pair = divmod(2 * j, DEPTH)
            parts = []
            for parity in range(2):
                at, slot = slot_of(pair + parity, core, quad)
                parts.append(in_buf[i, half * QUAD + at, slot].astype(jnp.float32))
            first, second = pair_lanes(*parts, low)
            out_buf[i, 0, :, lanes] = first.astype(jnp.bfloat16)
            out_buf[i, 1, :, lanes] = second.astype(jnp.bfloat16)
        write(i).start()

    for i in range(chunks):
        write(i).wait()


def body(field_state, forcing, inverses, owned_degree):
    fields, rows, group_cols = field_state.shape
    rad_count = lax.axis_size("rad")
    mode_count = lax.axis_size("mode")
    chips = rad_count // CORES
    spread = mode_count // DEPTH
    slots = rad_count * mode_count
    peers = chips * spread * QUAD
    whole_rows = rows * rad_count
    piece = group_cols // slots
    chip_cols = mode_count * piece
    core_cols = group_cols // CORES
    spacing = (R_OUTER - R_INNER) / (whole_rows - 1)

    def device(chip, core, x, z):
        return (chip * CORES + core) * mode_count + x * DEPTH + z

    quads = [
        [
            device(chip, core, x, (quad * QUAD + at + CORES * core) % DEPTH)
            for chip in range(chips)
            for x in range(spread)
            for at in range(QUAD)
        ]
        for core in range(CORES)
        for quad in range(DEPTH // QUAD)
    ]
    mirror = [
        (
            device(chip, core, x, (w + CORES * core) % DEPTH),
            device(chip, core, x, (DEPTH - 1 - w + CORES * core) % DEPTH),
        )
        for chip in range(chips)
        for core in range(CORES)
        for x in range(spread)
        for w in range(DEPTH)
    ]
    same_core = [[chip * CORES + core for chip in range(chips)] for core in range(CORES)]
    sibling = [(r, r ^ 1) for r in range(rad_count)]
    same_edge = [(r, r + 2) for r in range(1, rad_count - 2, 2)] + [
        (r, r - 2) for r in range(2, rad_count, 2)
    ]
    cross_edge = [(r, r + 1) for r in range(1, rad_count - 1, 2)] + [
        (r, r - 1) for r in range(2, rad_count, 2)
    ]

    core = lax.axis_index("rad") % CORES
    turned = [(lax.axis_index("mode") + DEPTH - CORES * c) % DEPTH for c in (core, 1 - core)]
    place = jnp.stack([core, turned[0] // QUAD, turned[1] // QUAD]).astype(jnp.int32)

    other_forcing = lax.ppermute(forcing, "rad", sibling)
    other_state = lax.ppermute(field_state, "rad", sibling)
    degree = jnp.broadcast_to(owned_degree.astype(jnp.float32)[:, None], (mode_count, LANES))
    degree = lax.all_to_all(degree, "mode", 0, 0, tiled=True)
    first_mirror = lax.ppermute(inverses[:1], AXES, mirror)
    edge = lax.dynamic_slice_in_dim(field_state, core * (rows - 1), 1, axis=1)
    same = lax.ppermute(edge, "rad", same_edge)
    cross = lax.ppermute(edge, "rad", cross_edge)
    degree, same, cross = lax.optimization_barrier((degree, same, cross))
    first_mirror, second_inverse, degree = lax.optimization_barrier(
        (first_mirror, inverses[1:], degree)
    )
    second_mirror = lax.ppermute(second_inverse, AXES, mirror)
    degree = jnp.broadcast_to(degree[None], (chips, mode_count, LANES))
    degree = lax.all_to_all(degree, "rad", 0, 0, axis_index_groups=same_core, tiled=True)

    anywhere = pl.BlockSpec(memory_space=pl.ANY)
    vmem = pl.BlockSpec(memory_space=pltpu.VMEM)
    smem = pl.BlockSpec(memory_space=pltpu.SMEM)
    packed = pl.pallas_call(
        functools.partial(right_side_kernel, spacing, piece),
        in_specs=[smem, vmem, vmem, vmem, anywhere, anywhere, anywhere, anywhere],
        out_specs=anywhere,
        out_shape=jax.ShapeDtypeStruct((peers, 2, CORES, rows, LANES), jnp.bfloat16),
        scratch_shapes=[
            pltpu.VMEM((chips, CORES, fields, rows, chip_cols), jnp.float32),
            pltpu.VMEM((chips, CORES, fields, rows, chip_cols), jnp.bfloat16),
            pltpu.VMEM((peers, 2, CORES, rows, LANES), jnp.bfloat16),
            pltpu.VMEM((fields, 3, CORES * rows, LANES), jnp.float32),
            pltpu.SemaphoreType.DMA((chips, 4)),
            pltpu.SemaphoreType.DMA((chips,)),
        ],
        compiler_params=pltpu.CompilerParams(vmem_limit_bytes=LARGE_VMEM),
        name="right_side",
    )(place, degree, same, cross, field_state, forcing, other_state, other_forcing)

    packed, second_mirror = lax.optimization_barrier((packed, second_mirror))
    packed = lax.all_to_all(packed, AXES, 0, 0, axis_index_groups=quads, tiled=True)

    groups = 2
    grouped = (chips, spread * QUAD, 2, CORES, rows, LANES)
    block = pl.BlockSpec((chips, groups, 2, CORES, rows, LANES), lambda i: (0, i, 0, 0, 0, 0))
    own_block = pl.BlockSpec((fields, 1, whole_rows, whole_rows), lambda i: (0, 0, 0, 0))
    mirror_block = pl.BlockSpec((1, 1, whole_rows, whole_rows), lambda i: (0, 0, 0, 0))
    solved = pl.pallas_call(
        functools.partial(solve_kernel, piece),
        grid=(spread * QUAD // groups,),
        in_specs=[own_block, mirror_block, mirror_block, block],
        out_specs=block,
        out_shape=jax.ShapeDtypeStruct(grouped, jnp.bfloat16),
        compiler_params=pltpu.CompilerParams(vmem_limit_bytes=SMALL_VMEM),
        name="solve",
    )(inverses, first_mirror, second_mirror, packed.reshape(grouped))

    solved = lax.all_to_all(
        solved.reshape(peers, 2, CORES, rows, LANES),
        AXES,
        0,
        0,
        axis_index_groups=quads,
        tiled=True,
    )

    def unpack(turn, solved, *partial):
        return pl.pallas_call(
            functools.partial(unpack_kernel, piece, turn),
            in_specs=[smem, anywhere] + [anywhere] * len(partial),
            out_specs=anywhere,
            out_shape=jax.ShapeDtypeStruct((fields, rows, group_cols), jnp.bfloat16),
            scratch_shapes=[
                pltpu.VMEM((chips, spread * QUAD, 2, rows, LANES), jnp.bfloat16),
                pltpu.VMEM((chips, fields, rows, chip_cols), jnp.bfloat16),
                pltpu.SemaphoreType.DMA((chips,)),
                pltpu.SemaphoreType.DMA((chips,)),
            ],
            input_output_aliases={2: 0} if partial else {},
            compiler_params=pltpu.CompilerParams(vmem_limit_bytes=SMALL_VMEM),
            cost_estimate=pl.CostEstimate(
                flops=2 * field_state.size, bytes_accessed=2 * field_state.size, transcendentals=0
            ),
            name="unpack_other" if turn else "unpack_own",
        )(place, solved, *partial)

    returned = lax.ppermute(solved, "rad", sibling)
    partial = unpack(0, solved)
    return unpack(1, returned, partial)


def solution(mesh):
    in_specs = (
        P(None, "rad", "mode"),
        P(None, "rad", "mode"),
        P(None, ("rad", "mode"), None, None),
        P(("rad", "mode")),
    )
    out_specs = P(None, "rad", "mode")
    return jax.shard_map(body, mesh=mesh, in_specs=in_specs, out_specs=out_specs, check_vma=False)
```

time: 545 us -> 178 us (0.33)
  waiting for transfers between devices: 248 us -> 6.5 us
  local copies, waits for them, and re-layouts: 134 us -> 4.1 us
  Pallas kernels: 0 us -> 17.9 us
  blocking collectives: 113 us -> 128 us
  starting transfers between devices: 33.7 us -> 19.5 us
  matrix products: 12.5 us -> 0 us
    all_to_all x4 -> x1, waiting for transfers between devices: 248 us -> 4.6 us  [body(): lax.all_to_all(degree, 'rad', 0, 0, axis_index_groups=same_core, tiled=True)]
    all_to_all x9 -> x0, local copies, waits for them, and re-layouts: 67.8 us -> none  [the longest x2 14.9 us: body(): lax.all_to_all(solved.reshape(2, whole_rows, 1, dev_cols), 'rad', split_a...]
    unnamed x8 -> x10, local copies, waits for them, and re-layouts: 33.5 us -> 0.61 us
    all_to_all x4 -> x1, starting transfers between devices: 33.7 us -> 4.22 us  [body(): lax.all_to_all(degree, 'rad', 0, 0, axis_index_groups=same_core, tiled=True)]
    reshape x4 -> x0, local copies, waits for them, and re-layouts: 22.1 us -> none  [the longest x1 7.47 us: body(): solved.reshape(2, whole_rows, 1, dev_cols)]
    pallas_call x0 -> x4, Pallas kernels: none -> 17.9 us  [the longest x1 6.79 us: body(): pl.pallas_call(functools.partial(right_side_kernel, spacing, piece), in_s...]
    ppermute x0 -> x7, starting transfers between devices: none -> 15.3 us  [the longest x1 3.24 us: body(): other_state = lax.ppermute(field_state, 'rad', sibling)]
    all_to_all x2 -> x3, blocking collectives: 113 us -> 128 us  [the longest x1 57 us: body(): lax.all_to_all(packed, AXES, 0, 0, axis_index_groups=quads, tiled=True)]
  transfers between devices with their start and end apart: 4 -> 8, of which waited for: 4 -> 2; matrix products, arithmetic and copies ran while one was open for 7% -> 2% of each run, Pallas kernels for 0% -> 6%
where the time goes in v2:
time: 178 us; the launch traced here: 177 us
  blocking collectives  128 us (72%)
  starting transfers between devices  19.5 us (11%)
  Pallas kernels  17.9 us (10%)
  waiting for transfers between devices  6.5 us (4%)
  local copies, waits for them, and re-layouts  4.1 us (2%)
    all_to_all x1, blocking collectives, body(): lax.all_to_all(packed, AXES, 0, 0, axis_index_groups=quads, tiled=True)  57 us
    all_to_all x1, blocking collectives, body(): lax.all_to_all(solved.reshape(peers, 2, CORES, rows, LANES), AXES, 0, 0,...  55.2 us
    all_to_all x1, blocking collectives, body(): degree = lax.all_to_all(degree, 'mode', 0, 0, tiled=True)  15.7 us
    pallas_call x1, Pallas kernels, body(): pl.pallas_call(functools.partial(right_side_kernel, spacing, piece), in_s...  6.79 us
    pallas_call x2, Pallas kernels, unpack(): pl.pallas_call(functools.partial(unpack_kernel, piece, turn), in_specs=[s...  6.04 us
    pallas_call x1, Pallas kernels, body(): pl.pallas_call(functools.partial(solve_kernel, piece), grid=(spread * QUA...  5.08 us
    all_to_all x1, waiting for transfers between devices, body(): lax.all_to_all(degree, 'rad', 0, 0, axis_index_groups=same_core, tiled=True)  4.6 us
    all_to_all x1, starting transfers between devices, body(): lax.all_to_all(degree, 'rad', 0, 0, axis_index_groups=same_core, tiled=True)  4.22 us
  transfers between devices with their start and end apart: 8, of which 2 were waited for; matrix products, arithmetic and copies ran while one was open for 2% of the time, Pallas kernels for 6%

profile of v2, /device:TPU:1, one launch (start us, length us, event | category | flops | bytes accessed | tf_op | source)
XLA Modules:
  0.0 177.4 jit_solution(3534499712866435010)
XLA Ops:
  0.0 3.2 %collective-permute-start.3 = (f32[2,40,16384]{2,1,0:T(8,128)}, f32[2,40,16384]{2,1,0:T(8,128)}, u32[]{:S(2)}, u32[]{:S(2)}) collective-permute-start(f32[2,40,16384]{2,1,0:T(8,128)} %own_ref.2), channel_id=1, source_target_pairs={{0,16},{16,0},{32,48},{48,32},{64,80},{80,64},{96,112},{112,96},{1... | collective-permute-start | bytes 15728648 | tf_op jit(solution)/shard_map/ppermute | solution.py:260
  3.2 1.5 fusion
  4.8 2.7 %collective-permute-start = (bf16[1,1,640,640]{3,2,1,0:T(8,128)(2,1)S(1)}, bf16[1,1,640,640]{3,2,1,0:T(8,128)(2,1)S(1)}, u32[]{:S(2)}, u32[]{:S(2)}) collective-permute-start(bf16[1,1,640,640]{3,2,1,0:T(8,128)(2,1)S(1)} %get-tuple-element.22), channel_id=1, source_target_pairs={{0,7},{1,6},{2,5},{3,4},{4,3},{5,2},{6,1},{7,0},{8,15},{9,14},{10,... | collective-permute-start | bytes 2457608 | tf_op jit(solution)/shard_map/ppermute | solution.py:263
  7.5 1.5 collective-permute-start.4
  9.0 1.3 constant_dynamic-slice_fusion
  10.3 3.1 %collective-permute-start.2 = (f32[2,1,16384]{2,1,0:T(1,128)S(1)}, f32[2,1,16384]{2,1,0:T(1,128)S(1)}, u32[]{:S(2)}, u32[]{:S(2)}) collective-permute-start(f32[2,1,16384]{2,1,0:T(1,128)S(1)} %constant_dynamic-slice_fusion), channel_id=1, source_target_pairs={{16,32},{48,64},{80,96},{112,128},{144,160},{176,192},{208,224},{3... | collective-permute-start | bytes 393224 | tf_op jit(solution)/shard_map/ppermute | solution.py:266
  13.4 3.2 %collective-permute-start.1 = (f32[2,1,16384]{2,1,0:T(1,128)S(1)}, f32[2,1,16384]{2,1,0:T(1,128)S(1)}, u32[]{:S(2)}, u32[]{:S(2)}) collective-permute-start(f32[2,1,16384]{2,1,0:T(1,128)S(1)} %constant_dynamic-slice_fusion), channel_id=1, source_target_pairs={{16,48},{48,80},{80,112},{112,144},{144,176},{176,208},{208,240},{... | collective-permute-start | bytes 393224 | tf_op jit(solution)/shard_map/ppermute | solution.py:265
  17.3 15.7 %all_to_all.24 = f32[16,1,128]{2,1,0:T(1,128)S(1)} all-to-all(f32[16,1,128]{2,1,0:T(1,128)S(1)} %broadcast_in_dim.7), channel_id=1, replica_groups=mesh['rad'=16,'mode'=16] {'mode'}, dimensions={0} | all-to-all | bytes 16384 | tf_op jit(solution)/shard_map/all_to_all | solution.py:262
  33.0 0.0 collective-permute-done.2.cross_ref
  33.0 0.0 copy-start.3
  33.0 0.0 collective-permute-done.1.same_ref
  33.0 0.0 copy-start.4
  33.0 0.0 collective-permute-done.refs_0_
  33.0 1.6 collective-permute-start.5
  34.6 0.6 broadcast_in_dim.16
  35.2 4.2 %all-to-all-start.1 = ((f32[8,16,128]{2,1,0:T(8,128)}), f32[8,16,128]{2,1,0:T(8,128)S(1)}, u32[]{:S(2)}, u32[]{:S(2)}) async-start(f32[8,16,128]{2,1,0:T(8,128)} %broadcast_in_dim.16), calls=%async_computation.1 | async-start | bytes 131072 | tf_op jit(solution)/shard_map/all_to_all | solution.py:273
  39.5 0.6 pad_add_fusion.place_ref
  40.1 4.6 %all-to-all-done.1.degree_ref = f32[8,16,128]{2,1,0:T(8,128)S(1)} async-done(((f32[8,16,128]{2,1,0:T(8,128)}), f32[8,16,128]{2,1,0:T(8,128)S(1)}, u32[]{:S(2)}, u32[]{:S(2)}) %all-to-all-start.1) | async-done | bytes 65568 | tf_op jit(solution)/shard_map/all_to_all | solution.py:273
  44.7 0.0 copy-start.2
  44.7 0.0 collective-permute-done.4.other_forcing_ref
  44.7 0.0 collective-permute-done.3.other_ref
  44.7 0.0 copy-done.3
  44.7 0.0 copy-done.4
  44.7 0.6 copy-done.2
  45.3 6.8 %right_side.1 = bf16[64,2,2,40,128]{4,3,2,1,0:T(8,128)(2,1)} custom-call(s32[3]{0:T(128)} %pad_add_fusion.place_ref, f32[8,16,128]{2,1,0:T(8,128)} %copy-done.2, f32[2,1,16384]{2,1,0:T(1,128)} %copy-done.4, f32[2,1,16384]{2,1,0:T(1,128)} %copy-done.3, f32[2,40,16384]{2,1,0:T(8,128)} %own_ref.2, bf16[2,40,16384]{2,1,0:T(8,128)(2,1)} %own_forcing_ref.1, ...), custom_call_target="tpu_custom_call" | custom-call | tf_op jit(solution)/shard_map/right_side/pallas_call | solution.py:278
  52.1 0.0 copy-start
  52.1 0.0 collective-permute-done.5.refs_1_
  52.1 57.0 %all_to_all.25 = bf16[64,2,2,40,128]{4,3,2,1,0:T(8,128)(2,1)S(1)} all-to-all(bf16[64,2,2,40,128]{4,3,2,1,0:T(8,128)(2,1)} %right_side.1), channel_id=1, replica_groups={{0,1,2,3,8,9,10,11,32,33,34,35,40,41,42,43,64,65,66,67,72,73,74,75,96,9..., dimensions={0} | all-to-all | bytes 5242880 | tf_op jit(solution)/shard_map/all_to_all | solution.py:296
  109.1 0.0 copy-done
  109.1 5.1 %solve.1 = bf16[8,8,2,2,40,128]{5,4,3,2,1,0:T(8,128)(2,1)S(1)} custom-call(bf16[2,1,640,640]{3,2,1,0:T(8,128)(2,1)S(1)} %copy-done, bf16[1,1,640,640]{3,2,1,0:T(8,128)(2,1)S(1)} %collective-permute-done.refs_0_, bf16[1,1,640,640]{3,2,1,0:T(8,128)(2,1)S(1)} %collective-permute-done.5.refs_1_, bf16[8,8,2,2,40,128]{5,4,3,2,1,0:T(8,128)(2,1)S(1)} %bitcast.7), custom_call_target="tpu_custom_call" | custom-call | tf_op jit(solution)/shard_map/solve/pallas_call | solution.py:303
  114.2 0.0 copy-start.1
  114.2 55.2 %all_to_all.26.solved_ref = bf16[64,2,2,40,128]{4,3,2,1,0:T(8,128)(2,1)S(1)} all-to-all(bf16[64,2,2,40,128]{4,3,2,1,0:T(8,128)(2,1)S(1)} %bitcast.8), channel_id=1, replica_groups={{0,1,2,3,8,9,10,11,32,33,34,35,40,41,42,43,64,65,66,67,72,73,74,75,96,9..., dimensions={0} | all-to-all | bytes 5242880 | tf_op jit(solution)/shard_map/all_to_all | solution.py:313
  169.4 0.0 collective-permute-start.6
  169.4 0.0 copy-done.1
  169.4 3.0 %unpack_own.1.refs_0_ = bf16[2,40,16384]{2,1,0:T(8,128)(2,1)} custom-call(s32[3]{0:T(128)S(1)} %copy-done.1, bf16[64,2,2,40,128]{4,3,2,1,0:T(8,128)(2,1)S(1)} %all_to_all.26.solved_ref), custom_call_target="tpu_custom_call" | custom-call | flops 2621440 | bytes 2621440 | tf_op jit(solution)/shard_map/unpack_own/pallas_call | solution.py:323
  172.5 1.9 %collective-permute-done.6.solved_ref = bf16[64,2,2,40,128]{4,3,2,1,0:T(8,128)(2,1)S(1)} collective-permute-done((bf16[64,2,2,40,128]{4,3,2,1,0:T(8,128)(2,1)S(1)}, bf16[64,2,2,40,128]{4,3,2,1,0:T(8,128)(2,1)S(1)}, u32[]{:S(2)}, u32[]{:S(2)}) %collective-permute-start.6) | collective-permute-done | bytes 2621472 | tf_op jit(solution)/shard_map/ppermute | solution.py:342
  174.3 3.0 %unpack_other.1 = bf16[2,40,16384]{2,1,0:T(8,128)(2,1)} custom-call(s32[3]{0:T(128)S(1)} %copy-done.1, bf16[64,2,2,40,128]{4,3,2,1,0:T(8,128)(2,1)S(1)} %collective-permute-done.6.solved_ref, bf16[2,40,16384]{2,1,0:T(8,128)(2,1)} %unpack_own.1.refs_0_), custom_call_target="tpu_custom_call", output_to_operand_aliasing={{}: (2, {})} | custom-call | flops 2621440 | bytes 2621440 | tf_op jit(solution)/shard_map/unpack_other/pallas_call | solution.py:323
  (1 shorter events, 0.0 us)
Async XLA Ops:
  0.0 44.7 %collective-permute-start.3 = (f32[2,40,16384]{2,1,0:T(8,128)}, f32[2,40,16384]{2,1,0:T(8,128)}, u32[]{:S(2)}, u32[]{:S(2)}) collective-permute-start(f32[2,40,16384]{2,1,0:T(8,128)} %own_ref.2), channel_id=1, source_target_pairs={{0,16},{16,0},{32,48},{48,32},{64,80},{80,64},{96,112},{112,96},{1... | collective-permute-start | bytes 15728648 | tf_op jit(solution)/shard_map/ppermute | solution.py:260
  4.8 28.2 %collective-permute-start = (bf16[1,1,640,640]{3,2,1,0:T(8,128)(2,1)S(1)}, bf16[1,1,640,640]{3,2,1,0:T(8,128)(2,1)S(1)}, u32[]{:S(2)}, u32[]{:S(2)}) collective-permute-start(bf16[1,1,640,640]{3,2,1,0:T(8,128)(2,1)S(1)} %get-tuple-element.22), channel_id=1, source_target_pairs={{0,7},{1,6},{2,5},{3,4},{4,3},{5,2},{6,1},{7,0},{8,15},{9,14},{10,... | collective-permute-start | bytes 2457608 | tf_op jit(solution)/shard_map/ppermute | solution.py:263
  7.5 37.2 %collective-permute-start.4 = (bf16[2,40,16384]{2,1,0:T(8,128)(2,1)}, bf16[2,40,16384]{2,1,0:T(8,128)(2,1)}, u32[]{:S(2)}, u32[]{:S(2)}) collective-permute-start(bf16[2,40,16384]{2,1,0:T(8,128)(2,1)} %own_forcing_ref.1), channel_id=1, source_target_pairs={{0,16},{16,0},{32,48},{48,32},{64,80},{80,64},{96,112},{112,96},{1... | collective-permute-start | bytes 7864328 | tf_op jit(solution)/shard_map/ppermute | solution.py:259
  10.3 22.7 %collective-permute-start.2 = (f32[2,1,16384]{2,1,0:T(1,128)S(1)}, f32[2,1,16384]{2,1,0:T(1,128)S(1)}, u32[]{:S(2)}, u32[]{:S(2)}) collective-permute-start(f32[2,1,16384]{2,1,0:T(1,128)S(1)} %constant_dynamic-slice_fusion), channel_id=1, source_target_pairs={{16,32},{48,64},{80,96},{112,128},{144,160},{176,192},{208,224},{3... | collective-permute-start | bytes 393224 | tf_op jit(solution)/shard_map/ppermute | solution.py:266
  13.4 19.6 %collective-permute-start.1 = (f32[2,1,16384]{2,1,0:T(1,128)S(1)}, f32[2,1,16384]{2,1,0:T(1,128)S(1)}, u32[]{:S(2)}, u32[]{:S(2)}) collective-permute-start(f32[2,1,16384]{2,1,0:T(1,128)S(1)} %constant_dynamic-slice_fusion), channel_id=1, source_target_pairs={{16,48},{48,80},{80,112},{112,144},{144,176},{176,208},{208,240},{... | collective-permute-start | bytes 393224 | tf_op jit(solution)/shard_map/ppermute | solution.py:265
  33.0 11.7 %copy-start.3 = (f32[2,1,16384]{2,1,0:T(1,128)}, f32[2,1,16384]{2,1,0:T(1,128)S(1)}, u32[]{:S(2)}) copy-start(f32[2,1,16384]{2,1,0:T(1,128)S(1)} %collective-permute-done.2.cross_ref) | copy-start | bytes 393220
  33.0 11.7 %copy-start.4 = (f32[2,1,16384]{2,1,0:T(1,128)}, f32[2,1,16384]{2,1,0:T(1,128)S(1)}, u32[]{:S(2)}) copy-start(f32[2,1,16384]{2,1,0:T(1,128)S(1)} %collective-permute-done.1.same_ref) | copy-start | bytes 393220
  33.0 19.1 %collective-permute-start.5 = (bf16[1,1,640,640]{3,2,1,0:T(8,128)(2,1)S(1)}, bf16[1,1,640,640]{3,2,1,0:T(8,128)(2,1)S(1)}, u32[]{:S(2)}, u32[]{:S(2)}) collective-permute-start(bf16[1,1,640,640]{3,2,1,0:T(8,128)(2,1)S(1)} %get-tuple-element.18), channel_id=1, source_target_pairs={{0,7},{1,6},{2,5},{3,4},{4,3},{5,2},{6,1},{7,0},{8,15},{9,14},{10,... | collective-permute-start | bytes 2457608 | tf_op jit(solution)/shard_map/ppermute | solution.py:271
  35.2 9.4 %all-to-all-start.1 = ((f32[8,16,128]{2,1,0:T(8,128)}), f32[8,16,128]{2,1,0:T(8,128)S(1)}, u32[]{:S(2)}, u32[]{:S(2)}) async-start(f32[8,16,128]{2,1,0:T(8,128)} %broadcast_in_dim.16), calls=%async_computation.1 | async-start | bytes 131072 | tf_op jit(solution)/shard_map/all_to_all | solution.py:273
  44.7 0.6 copy-start.2
  52.1 57.0 %copy-start = (bf16[2,1,640,640]{3,2,1,0:T(8,128)(2,1)S(1)}, bf16[2,1,640,640]{3,2,1,0:T(8,128)(2,1)}, u32[]{:S(2)}) copy-start(bf16[2,1,640,640]{3,2,1,0:T(8,128)(2,1)} %own_ref.3) | copy-start | bytes 4915204
  114.2 55.2 %copy-start.1 = (s32[3]{0:T(128)S(1)}, s32[3]{0:T(128)}, u32[]{:S(2)}) copy-start(s32[3]{0:T(128)} %pad_add_fusion.place_ref) | copy-start | bytes 40
  169.4 4.9 %collective-permute-start.6 = (bf16[64,2,2,40,128]{4,3,2,1,0:T(8,128)(2,1)S(1)}, bf16[64,2,2,40,128]{4,3,2,1,0:T(8,128)(2,1)S(1)}, u32[]{:S(2)}, u32[]{:S(2)}) collective-permute-start(bf16[64,2,2,40,128]{4,3,2,1,0:T(8,128)(2,1)S(1)} %all_to_all.26.solved_ref), channel_id=1, source_target_pairs={{0,16},{16,0},{32,48},{48,32},{64,80},{80,64},{96,112},{112,96},{1... | collective-permute-start | bytes 7864328 | tf_op jit(solution)/shard_map/ppermute | solution.py:342

commit v3 on v2

--- a/solution.py
+++ b/solution.py
@@ -16,6 +16,7 @@
 CORES = 2
 DEPTH = 8
 QUAD = DEPTH // 2
+AHEAD = 3
 SMALL_VMEM = 24 * 1024 * 1024
 LARGE_VMEM = 56 * 1024 * 1024
 
@@ -73,7 +74,7 @@
         block = pl.ds(i * peers, peers)
         return pltpu.make_async_copy(out_buf.at[block], out_ref.at[block], out_sem.at[i])
 
-    for i in range(chunks):
+    for i in range(AHEAD):
         for copy in reads(i):
             copy.start()
 
@@ -91,6 +92,11 @@
 
     @pl.loop(0, chunks)
     def _(i):
+        @pl.when(i + AHEAD < chunks)
+        def _():
+            for copy in reads(i + AHEAD):
+                copy.start()
+
         for copy in reads(i):
             copy.wait()
         for j in range(cols // LANES):
@@ -142,28 +148,31 @@
     *mirror_refs, side_ref, out_ref = refs
     chips, groups, slots, cores, rows, _ = side_ref.shape
     whole = chips * cores * rows
-    low = lax.broadcasted_iota(jnp.int32, (whole, groups * LANES), 1) % LANES < piece
+    low = lax.broadcasted_iota(jnp.int32, (whole, LANES), 1) < piece
     own = [own_ref[f, 0] for f in range(own_ref.shape[0])]
     mirror = [ref[0, 0] for ref in mirror_refs]
     for slot, inverse in enumerate((own, mirror)):
-        side = jnp.concatenate(
-            [
-                side_ref[:, g, slot].astype(jnp.float32).reshape(whole, LANES).astype(jnp.bfloat16)
-                for g in range(groups)
-            ],
-            axis=1,
-        )
-        solved = jnp.where(
-            low,
-            jnp.dot(inverse[0], side, preferred_element_type=jnp.float32),
-            jnp.dot(inverse[1], side, preferred_element_type=jnp.float32),
-        )
-        for g in range(groups):
-            out_ref[:, g, slot] = (
-                solved[:, g * LANES : (g + 1) * LANES]
-                .reshape(chips, cores, rows, LANES)
-                .astype(jnp.bfloat16)
+        pairs = []
+        for g in range(0, groups, 2):
+            packed = [
+                side_ref[:, g + n, slot].astype(jnp.float32).reshape(whole, LANES) for n in range(2)
+            ]
+            pairs.append(pair_lanes(*packed, low))
+        solved = [
+            jnp.dot(
+                inverse[f],
+                jnp.concatenate([pair[f].astype(jnp.bfloat16) for pair in pairs], axis=1),
+                preferred_element_type=jnp.float32,
             )
+            for f in range(2)
+        ]
+        for g in range(0, groups, 2):
+            lanes = slice(g // 2 * LANES, (g // 2 + 1) * LANES)
+            packed = pair_lanes(solved[0][:, lanes], solved[1][:, lanes], low)
+            for n in range(2):
+                out_ref[:, g + n, slot] = (
+                    packed[n].reshape(chips, cores, rows, LANES).astype(jnp.bfloat16)
+                )
 
 
 def unpack_kernel(piece, turn, place_ref, solved_ref, *refs):
@@ -295,7 +304,7 @@
     packed, second_mirror = lax.optimization_barrier((packed, second_mirror))
     packed = lax.all_to_all(packed, AXES, 0, 0, axis_index_groups=quads, tiled=True)
 
-    groups = 2
+    groups = 4
     grouped = (chips, spread * QUAD, 2, CORES, rows, LANES)
     block = pl.BlockSpec((chips, groups, 2, CORES, rows, LANES), lambda i: (0, i, 0, 0, 0, 0))
     own_block = pl.BlockSpec((fields, 1, whole_rows, whole_rows), lambda i: (0, 0, 0, 0))

time: 178 us -> 176 us (0.989)
  Pallas kernels: 17.9 us -> 16.1 us
    pallas_call x1, Pallas kernels: 5.08 us -> 3.18 us  [body(): pl.pallas_call(functools.partial(solve_kernel, piece), grid=(spread * QUA...]
where the time goes in v3:
time: 176 us; the launch traced here: 175 us
  blocking collectives  128 us (73%)
  starting transfers between devices  19.5 us (11%)
  Pallas kernels  16.1 us (9%)
  waiting for transfers between devices  6.5 us (4%)
  local copies, waits for them, and re-layouts  4.1 us (2%)
    all_to_all x1, blocking collectives, body(): lax.all_to_all(packed, AXES, 0, 0, axis_index_groups=quads, tiled=True)  56.9 us
    all_to_all x1, blocking collectives, body(): lax.all_to_all(solved.reshape(peers, 2, CORES, rows, LANES), AXES, 0, 0,...  55.2 us
    all_to_all x1, blocking collectives, body(): degree = lax.all_to_all(degree, 'mode', 0, 0, tiled=True)  15.7 us
    pallas_call x1, Pallas kernels, body(): pl.pallas_call(functools.partial(right_side_kernel, spacing, piece), in_s...  6.9 us
    pallas_call x2, Pallas kernels, unpack(): pl.pallas_call(functools.partial(unpack_kernel, piece, turn), in_specs=[s...  6.04 us
    all_to_all x1, waiting for transfers between devices, body(): lax.all_to_all(degree, 'rad', 0, 0, axis_index_groups=same_core, tiled=True)  4.6 us
    all_to_all x1, starting transfers between devices, body(): lax.all_to_all(degree, 'rad', 0, 0, axis_index_groups=same_core, tiled=True)  4.22 us
  transfers between devices with their start and end apart: 8, of which 2 were waited for; matrix products, arithmetic and copies ran while one was open for 2% of the time, Pallas kernels for 6%

profile of v3, /device:TPU:1, one launch (start us, length us, event | category | flops | bytes accessed | tf_op | source)
XLA Modules:
  0.0 175.5 jit_solution(2325842792847078268)
XLA Ops:
  0.0 3.2 %collective-permute-start.3 = (f32[2,40,16384]{2,1,0:T(8,128)}, f32[2,40,16384]{2,1,0:T(8,128)}, u32[]{:S(2)}, u32[]{:S(2)}) collective-permute-start(f32[2,40,16384]{2,1,0:T(8,128)} %own_ref.2), channel_id=1, source_target_pairs={{0,16},{16,0},{32,48},{48,32},{64,80},{80,64},{96,112},{112,96},{1... | collective-permute-start | bytes 15728648 | tf_op jit(solution)/shard_map/ppermute | solution.py:269
  3.2 1.5 fusion
  4.8 2.7 %collective-permute-start = (bf16[1,1,640,640]{3,2,1,0:T(8,128)(2,1)S(1)}, bf16[1,1,640,640]{3,2,1,0:T(8,128)(2,1)S(1)}, u32[]{:S(2)}, u32[]{:S(2)}) collective-permute-start(bf16[1,1,640,640]{3,2,1,0:T(8,128)(2,1)S(1)} %get-tuple-element.22), channel_id=1, source_target_pairs={{0,7},{1,6},{2,5},{3,4},{4,3},{5,2},{6,1},{7,0},{8,15},{9,14},{10,... | collective-permute-start | bytes 2457608 | tf_op jit(solution)/shard_map/ppermute | solution.py:272
  7.5 1.5 collective-permute-start.4
  9.0 1.3 constant_dynamic-slice_fusion
  10.3 3.1 %collective-permute-start.2 = (f32[2,1,16384]{2,1,0:T(1,128)S(1)}, f32[2,1,16384]{2,1,0:T(1,128)S(1)}, u32[]{:S(2)}, u32[]{:S(2)}) collective-permute-start(f32[2,1,16384]{2,1,0:T(1,128)S(1)} %constant_dynamic-slice_fusion), channel_id=1, source_target_pairs={{16,32},{48,64},{80,96},{112,128},{144,160},{176,192},{208,224},{3... | collective-permute-start | bytes 393224 | tf_op jit(solution)/shard_map/ppermute | solution.py:275
  13.4 3.2 %collective-permute-start.1 = (f32[2,1,16384]{2,1,0:T(1,128)S(1)}, f32[2,1,16384]{2,1,0:T(1,128)S(1)}, u32[]{:S(2)}, u32[]{:S(2)}) collective-permute-start(f32[2,1,16384]{2,1,0:T(1,128)S(1)} %constant_dynamic-slice_fusion), channel_id=1, source_target_pairs={{16,48},{48,80},{80,112},{112,144},{144,176},{176,208},{208,240},{... | collective-permute-start | bytes 393224 | tf_op jit(solution)/shard_map/ppermute | solution.py:274
  17.3 15.7 %all_to_all.24 = f32[16,1,128]{2,1,0:T(1,128)S(1)} all-to-all(f32[16,1,128]{2,1,0:T(1,128)S(1)} %broadcast_in_dim.7), channel_id=1, replica_groups=mesh['rad'=16,'mode'=16] {'mode'}, dimensions={0} | all-to-all | bytes 16384 | tf_op jit(solution)/shard_map/all_to_all | solution.py:271
  33.0 0.0 collective-permute-done.2.cross_ref
  33.0 0.0 copy-start.3
  33.0 0.0 collective-permute-done.1.same_ref
  33.0 0.0 copy-start.4
  33.0 0.0 collective-permute-done.refs_0_
  33.0 1.6 collective-permute-start.5
  34.6 0.6 broadcast_in_dim.16
  35.2 4.2 %all-to-all-start.1 = ((f32[8,16,128]{2,1,0:T(8,128)}), f32[8,16,128]{2,1,0:T(8,128)S(1)}, u32[]{:S(2)}, u32[]{:S(2)}) async-start(f32[8,16,128]{2,1,0:T(8,128)} %broadcast_in_dim.16), calls=%async_computation.1 | async-start | bytes 131072 | tf_op jit(solution)/shard_map/all_to_all | solution.py:282
  39.5 0.6 pad_add_fusion.place_ref
  40.1 4.6 %all-to-all-done.1.degree_ref = f32[8,16,128]{2,1,0:T(8,128)S(1)} async-done(((f32[8,16,128]{2,1,0:T(8,128)}), f32[8,16,128]{2,1,0:T(8,128)S(1)}, u32[]{:S(2)}, u32[]{:S(2)}) %all-to-all-start.1) | async-done | bytes 65568 | tf_op jit(solution)/shard_map/all_to_all | solution.py:282
  44.7 0.0 copy-start.2
  44.7 0.0 collective-permute-done.4.other_forcing_ref
  44.7 0.0 collective-permute-done.3.other_ref
  44.7 0.0 copy-done.3
  44.7 0.0 copy-done.4
  44.7 0.6 copy-done.2
  45.3 6.9 %right_side.1 = bf16[64,2,2,40,128]{4,3,2,1,0:T(8,128)(2,1)} custom-call(s32[3]{0:T(128)} %pad_add_fusion.place_ref, f32[8,16,128]{2,1,0:T(8,128)} %copy-done.2, f32[2,1,16384]{2,1,0:T(1,128)} %copy-done.4, f32[2,1,16384]{2,1,0:T(1,128)} %copy-done.3, f32[2,40,16384]{2,1,0:T(8,128)} %own_ref.2, bf16[2,40,16384]{2,1,0:T(8,128)(2,1)} %own_forcing_ref.1, ...), custom_call_target="tpu_custom_call" | custom-call | tf_op jit(solution)/shard_map/right_side/pallas_call | solution.py:287
  52.2 0.0 copy-start
  52.2 0.0 collective-permute-done.5.refs_1_
  52.2 56.9 %all_to_all.25 = bf16[64,2,2,40,128]{4,3,2,1,0:T(8,128)(2,1)S(1)} all-to-all(bf16[64,2,2,40,128]{4,3,2,1,0:T(8,128)(2,1)} %right_side.1), channel_id=1, replica_groups={{0,1,2,3,8,9,10,11,32,33,34,35,40,41,42,43,64,65,66,67,72,73,74,75,96,9..., dimensions={0} | all-to-all | bytes 5242880 | tf_op jit(solution)/shard_map/all_to_all | solution.py:305
  109.1 0.0 copy-done
  109.1 3.2 %solve.1 = bf16[8,8,2,2,40,128]{5,4,3,2,1,0:T(8,128)(2,1)S(1)} custom-call(bf16[2,1,640,640]{3,2,1,0:T(8,128)(2,1)S(1)} %copy-done, bf16[1,1,640,640]{3,2,1,0:T(8,128)(2,1)S(1)} %collective-permute-done.refs_0_, bf16[1,1,640,640]{3,2,1,0:T(8,128)(2,1)S(1)} %collective-permute-done.5.refs_1_, bf16[8,8,2,2,40,128]{5,4,3,2,1,0:T(8,128)(2,1)S(1)} %bitcast.7), custom_call_target="tpu_custom_call" | custom-call | tf_op jit(solution)/shard_map/solve/pallas_call | solution.py:312
  112.3 0.0 copy-start.1
  112.3 55.2 %all_to_all.26.solved_ref = bf16[64,2,2,40,128]{4,3,2,1,0:T(8,128)(2,1)S(1)} all-to-all(bf16[64,2,2,40,128]{4,3,2,1,0:T(8,128)(2,1)S(1)} %bitcast.8), channel_id=1, replica_groups={{0,1,2,3,8,9,10,11,32,33,34,35,40,41,42,43,64,65,66,67,72,73,74,75,96,9..., dimensions={0} | all-to-all | bytes 5242880 | tf_op jit(solution)/shard_map/all_to_all | solution.py:322
  167.5 0.0 collective-permute-start.6
  167.5 0.0 copy-done.1
  167.5 3.0 %unpack_own.1.refs_0_ = bf16[2,40,16384]{2,1,0:T(8,128)(2,1)} custom-call(s32[3]{0:T(128)S(1)} %copy-done.1, bf16[64,2,2,40,128]{4,3,2,1,0:T(8,128)(2,1)S(1)} %all_to_all.26.solved_ref), custom_call_target="tpu_custom_call" | custom-call | flops 2621440 | bytes 2621440 | tf_op jit(solution)/shard_map/unpack_own/pallas_call | solution.py:332
  170.6 1.9 %collective-permute-done.6.solved_ref = bf16[64,2,2,40,128]{4,3,2,1,0:T(8,128)(2,1)S(1)} collective-permute-done((bf16[64,2,2,40,128]{4,3,2,1,0:T(8,128)(2,1)S(1)}, bf16[64,2,2,40,128]{4,3,2,1,0:T(8,128)(2,1)S(1)}, u32[]{:S(2)}, u32[]{:S(2)}) %collective-permute-start.6) | collective-permute-done | bytes 2621472 | tf_op jit(solution)/shard_map/ppermute | solution.py:351
  172.4 3.0 %unpack_other.1 = bf16[2,40,16384]{2,1,0:T(8,128)(2,1)} custom-call(s32[3]{0:T(128)S(1)} %copy-done.1, bf16[64,2,2,40,128]{4,3,2,1,0:T(8,128)(2,1)S(1)} %collective-permute-done.6.solved_ref, bf16[2,40,16384]{2,1,0:T(8,128)(2,1)} %unpack_own.1.refs_0_), custom_call_target="tpu_custom_call", output_to_operand_aliasing={{}: (2, {})} | custom-call | flops 2621440 | bytes 2621440 | tf_op jit(solution)/shard_map/unpack_other/pallas_call | solution.py:332
  (1 shorter events, 0.0 us)
Async XLA Ops:
  0.0 44.7 %collective-permute-start.3 = (f32[2,40,16384]{2,1,0:T(8,128)}, f32[2,40,16384]{2,1,0:T(8,128)}, u32[]{:S(2)}, u32[]{:S(2)}) collective-permute-start(f32[2,40,16384]{2,1,0:T(8,128)} %own_ref.2), channel_id=1, source_target_pairs={{0,16},{16,0},{32,48},{48,32},{64,80},{80,64},{96,112},{112,96},{1... | collective-permute-start | bytes 15728648 | tf_op jit(solution)/shard_map/ppermute | solution.py:269
  4.8 28.2 %collective-permute-start = (bf16[1,1,640,640]{3,2,1,0:T(8,128)(2,1)S(1)}, bf16[1,1,640,640]{3,2,1,0:T(8,128)(2,1)S(1)}, u32[]{:S(2)}, u32[]{:S(2)}) collective-permute-start(bf16[1,1,640,640]{3,2,1,0:T(8,128)(2,1)S(1)} %get-tuple-element.22), channel_id=1, source_target_pairs={{0,7},{1,6},{2,5},{3,4},{4,3},{5,2},{6,1},{7,0},{8,15},{9,14},{10,... | collective-permute-start | bytes 2457608 | tf_op jit(solution)/shard_map/ppermute | solution.py:272
  7.5 37.2 %collective-permute-start.4 = (bf16[2,40,16384]{2,1,0:T(8,128)(2,1)}, bf16[2,40,16384]{2,1,0:T(8,128)(2,1)}, u32[]{:S(2)}, u32[]{:S(2)}) collective-permute-start(bf16[2,40,16384]{2,1,0:T(8,128)(2,1)} %own_forcing_ref.1), channel_id=1, source_target_pairs={{0,16},{16,0},{32,48},{48,32},{64,80},{80,64},{96,112},{112,96},{1... | collective-permute-start | bytes 7864328 | tf_op jit(solution)/shard_map/ppermute | solution.py:268
  10.3 22.7 %collective-permute-start.2 = (f32[2,1,16384]{2,1,0:T(1,128)S(1)}, f32[2,1,16384]{2,1,0:T(1,128)S(1)}, u32[]{:S(2)}, u32[]{:S(2)}) collective-permute-start(f32[2,1,16384]{2,1,0:T(1,128)S(1)} %constant_dynamic-slice_fusion), channel_id=1, source_target_pairs={{16,32},{48,64},{80,96},{112,128},{144,160},{176,192},{208,224},{3... | collective-permute-start | bytes 393224 | tf_op jit(solution)/shard_map/ppermute | solution.py:275
  13.4 19.6 %collective-permute-start.1 = (f32[2,1,16384]{2,1,0:T(1,128)S(1)}, f32[2,1,16384]{2,1,0:T(1,128)S(1)}, u32[]{:S(2)}, u32[]{:S(2)}) collective-permute-start(f32[2,1,16384]{2,1,0:T(1,128)S(1)} %constant_dynamic-slice_fusion), channel_id=1, source_target_pairs={{16,48},{48,80},{80,112},{112,144},{144,176},{176,208},{208,240},{... | collective-permute-start | bytes 393224 | tf_op jit(solution)/shard_map/ppermute | solution.py:274
  33.0 11.7 %copy-start.3 = (f32[2,1,16384]{2,1,0:T(1,128)}, f32[2,1,16384]{2,1,0:T(1,128)S(1)}, u32[]{:S(2)}) copy-start(f32[2,1,16384]{2,1,0:T(1,128)S(1)} %collective-permute-done.2.cross_ref) | copy-start | bytes 393220
  33.0 11.7 %copy-start.4 = (f32[2,1,16384]{2,1,0:T(1,128)}, f32[2,1,16384]{2,1,0:T(1,128)S(1)}, u32[]{:S(2)}) copy-start(f32[2,1,16384]{2,1,0:T(1,128)S(1)} %collective-permute-done.1.same_ref) | copy-start | bytes 393220
  33.0 19.2 %collective-permute-start.5 = (bf16[1,1,640,640]{3,2,1,0:T(8,128)(2,1)S(1)}, bf16[1,1,640,640]{3,2,1,0:T(8,128)(2,1)S(1)}, u32[]{:S(2)}, u32[]{:S(2)}) collective-permute-start(bf16[1,1,640,640]{3,2,1,0:T(8,128)(2,1)S(1)} %get-tuple-element.18), channel_id=1, source_target_pairs={{0,7},{1,6},{2,5},{3,4},{4,3},{5,2},{6,1},{7,0},{8,15},{9,14},{10,... | collective-permute-start | bytes 2457608 | tf_op jit(solution)/shard_map/ppermute | solution.py:280
  35.2 9.4 %all-to-all-start.1 = ((f32[8,16,128]{2,1,0:T(8,128)}), f32[8,16,128]{2,1,0:T(8,128)S(1)}, u32[]{:S(2)}, u32[]{:S(2)}) async-start(f32[8,16,128]{2,1,0:T(8,128)} %broadcast_in_dim.16), calls=%async_computation.1 | async-start | bytes 131072 | tf_op jit(solution)/shard_map/all_to_all | solution.py:282
  44.7 0.6 copy-start.2
  52.2 56.9 %copy-start = (bf16[2,1,640,640]{3,2,1,0:T(8,128)(2,1)S(1)}, bf16[2,1,640,640]{3,2,1,0:T(8,128)(2,1)}, u32[]{:S(2)}) copy-start(bf16[2,1,640,640]{3,2,1,0:T(8,128)(2,1)} %own_ref.3) | copy-start | bytes 4915204
  112.3 55.2 %copy-start.1 = (s32[3]{0:T(128)S(1)}, s32[3]{0:T(128)}, u32[]{:S(2)}) copy-start(s32[3]{0:T(128)} %pad_add_fusion.place_ref) | copy-start | bytes 40
  167.5 4.9 %collective-permute-start.6 = (bf16[64,2,2,40,128]{4,3,2,1,0:T(8,128)(2,1)S(1)}, bf16[64,2,2,40,128]{4,3,2,1,0:T(8,128)(2,1)S(1)}, u32[]{:S(2)}, u32[]{:S(2)}) collective-permute-start(bf16[64,2,2,40,128]{4,3,2,1,0:T(8,128)(2,1)S(1)} %all_to_all.26.solved_ref), channel_id=1, source_target_pairs={{0,16},{16,0},{32,48},{48,32},{64,80},{80,64},{96,112},{112,96},{1... | collective-permute-start | bytes 7864328 | tf_op jit(solution)/shard_map/ppermute | solution.py:351

commit v4 on v3

--- a/solution.py
+++ b/solution.py
@@ -149,20 +149,24 @@
     chips, groups, slots, cores, rows, _ = side_ref.shape
     whole = chips * cores * rows
     low = lax.broadcasted_iota(jnp.int32, (whole, LANES), 1) < piece
-    own = [own_ref[f, 0] for f in range(own_ref.shape[0])]
-    mirror = [ref[0, 0] for ref in mirror_refs]
-    for slot, inverse in enumerate((own, mirror)):
+    for slot, parts in enumerate(([own_ref], mirror_refs)):
         pairs = []
         for g in range(0, groups, 2):
             packed = [
                 side_ref[:, g + n, slot].astype(jnp.float32).reshape(whole, LANES) for n in range(2)
             ]
             pairs.append(pair_lanes(*packed, low))
+        sides = [
+            jnp.concatenate([pair[f].astype(jnp.bfloat16) for pair in pairs], axis=1)
+            for f in range(2)
+        ]
         solved = [
-            jnp.dot(
-                inverse[f],
-                jnp.concatenate([pair[f].astype(jnp.bfloat16) for pair in pairs], axis=1),
-                preferred_element_type=jnp.float32,
+            jnp.concatenate(
+                [
+                    jnp.dot(part[f, 0], sides[f], preferred_element_type=jnp.float32)
+                    for part in parts
+                ],
+                axis=0,
             )
             for f in range(2)
         ]
@@ -265,17 +269,18 @@
     turned = [(lax.axis_index("mode") + DEPTH - CORES * c) % DEPTH for c in (core, 1 - core)]
     place = jnp.stack([core, turned[0] // QUAD, turned[1] // QUAD]).astype(jnp.int32)
 
+    early = whole_rows // 2
     other_forcing = lax.ppermute(forcing, "rad", sibling)
     other_state = lax.ppermute(field_state, "rad", sibling)
     degree = jnp.broadcast_to(owned_degree.astype(jnp.float32)[:, None], (mode_count, LANES))
     degree = lax.all_to_all(degree, "mode", 0, 0, tiled=True)
-    first_mirror = lax.ppermute(inverses[:1], AXES, mirror)
+    first_mirror = lax.ppermute(inverses[:, :, :early], AXES, mirror)
     edge = lax.dynamic_slice_in_dim(field_state, core * (rows - 1), 1, axis=1)
     same = lax.ppermute(edge, "rad", same_edge)
     cross = lax.ppermute(edge, "rad", cross_edge)
     degree, same, cross = lax.optimization_barrier((degree, same, cross))
     first_mirror, second_inverse, degree = lax.optimization_barrier(
-        (first_mirror, inverses[1:], degree)
+        (first_mirror, inverses[:, :, early:], degree)
     )
     second_mirror = lax.ppermute(second_inverse, AXES, mirror)
     degree = jnp.broadcast_to(degree[None], (chips, mode_count, LANES))
@@ -308,11 +313,14 @@
     grouped = (chips, spread * QUAD, 2, CORES, rows, LANES)
     block = pl.BlockSpec((chips, groups, 2, CORES, rows, LANES), lambda i: (0, i, 0, 0, 0, 0))
     own_block = pl.BlockSpec((fields, 1, whole_rows, whole_rows), lambda i: (0, 0, 0, 0))
-    mirror_block = pl.BlockSpec((1, 1, whole_rows, whole_rows), lambda i: (0, 0, 0, 0))
+    mirror_blocks = [
+        pl.BlockSpec((fields, 1, height, whole_rows), lambda i: (0, 0, 0, 0))
+        for height in (early, whole_rows - early)
+    ]
     solved = pl.pallas_call(
         functools.partial(solve_kernel, piece),
         grid=(spread * QUAD // groups,),
-        in_specs=[own_block, mirror_block, mirror_block, block],
+        in_specs=[own_block, *mirror_blocks, block],
         out_specs=block,
         out_shape=jax.ShapeDtypeStruct(grouped, jnp.bfloat16),
         compiler_params=pltpu.CompilerParams(vmem_limit_bytes=SMALL_VMEM),

time: 176 us -> 176 us (level)
  no operation moved by 1% of the time
where the time goes in v4:
time: 176 us
  blocking collectives  128 us (73%)
  starting transfers between devices  19.5 us (11%)
  Pallas kernels  16.2 us (9%)
  waiting for transfers between devices  6.5 us (4%)
  local copies, waits for them, and re-layouts  4.1 us (2%)
    all_to_all x1, blocking collectives, body(): lax.all_to_all(packed, AXES, 0, 0, axis_index_groups=quads, tiled=True)  56.9 us
    all_to_all x1, blocking collectives, body(): lax.all_to_all(solved.reshape(peers, 2, CORES, rows, LANES), AXES, 0, 0,...  55.2 us
    all_to_all x1, blocking collectives, body(): degree = lax.all_to_all(degree, 'mode', 0, 0, tiled=True)  15.7 us
    pallas_call x1, Pallas kernels, body(): pl.pallas_call(functools.partial(right_side_kernel, spacing, piece), in_s...  6.9 us
    pallas_call x2, Pallas kernels, unpack(): pl.pallas_call(functools.partial(unpack_kernel, piece, turn), in_specs=[s...  6.04 us
    all_to_all x1, waiting for transfers between devices, body(): lax.all_to_all(degree, 'rad', 0, 0, axis_index_groups=same_core, tiled=True)  4.6 us
    all_to_all x1, starting transfers between devices, body(): lax.all_to_all(degree, 'rad', 0, 0, axis_index_groups=same_core, tiled=True)  4.22 us
  transfers between devices with their start and end apart: 8, of which 2 were waited for; matrix products, arithmetic and copies ran while one was open for 2% of the time, Pallas kernels for 6%

profile of v4, /device:TPU:1, one launch (start us, length us, event | category | flops | bytes accessed | tf_op | source)
XLA Modules:
  0.0 175.5 jit_solution(14726823184781409004)
XLA Ops:
  0.0 3.2 %collective-permute-start.3 = (f32[2,40,16384]{2,1,0:T(8,128)}, f32[2,40,16384]{2,1,0:T(8,128)}, u32[]{:S(2)}, u32[]{:S(2)}) collective-permute-start(f32[2,40,16384]{2,1,0:T(8,128)} %own_ref.2), channel_id=1, source_target_pairs={{0,16},{16,0},{32,48},{48,32},{64,80},{80,64},{96,112},{112,96},{1... | collective-permute-start | bytes 15728648 | tf_op jit(solution)/shard_map/ppermute | solution.py:274
  3.2 1.5 fusion
  4.8 2.7 %collective-permute-start = (bf16[2,1,320,640]{3,2,1,0:T(8,128)(2,1)S(1)}, bf16[2,1,320,640]{3,2,1,0:T(8,128)(2,1)S(1)}, u32[]{:S(2)}, u32[]{:S(2)}) collective-permute-start(bf16[2,1,320,640]{3,2,1,0:T(8,128)(2,1)S(1)} %get-tuple-element.22), channel_id=1, source_target_pairs={{0,7},{1,6},{2,5},{3,4},{4,3},{5,2},{6,1},{7,0},{8,15},{9,14},{10,... | collective-permute-start | bytes 2457608 | tf_op jit(solution)/shard_map/ppermute | solution.py:277
  7.5 1.5 collective-permute-start.4
  9.0 1.3 constant_dynamic-slice_fusion
  10.3 3.1 %collective-permute-start.2 = (f32[2,1,16384]{2,1,0:T(1,128)S(1)}, f32[2,1,16384]{2,1,0:T(1,128)S(1)}, u32[]{:S(2)}, u32[]{:S(2)}) collective-permute-start(f32[2,1,16384]{2,1,0:T(1,128)S(1)} %constant_dynamic-slice_fusion), channel_id=1, source_target_pairs={{16,32},{48,64},{80,96},{112,128},{144,160},{176,192},{208,224},{3... | collective-permute-start | bytes 393224 | tf_op jit(solution)/shard_map/ppermute | solution.py:280
  13.4 3.2 %collective-permute-start.1 = (f32[2,1,16384]{2,1,0:T(1,128)S(1)}, f32[2,1,16384]{2,1,0:T(1,128)S(1)}, u32[]{:S(2)}, u32[]{:S(2)}) collective-permute-start(f32[2,1,16384]{2,1,0:T(1,128)S(1)} %constant_dynamic-slice_fusion), channel_id=1, source_target_pairs={{16,48},{48,80},{80,112},{112,144},{144,176},{176,208},{208,240},{... | collective-permute-start | bytes 393224 | tf_op jit(solution)/shard_map/ppermute | solution.py:279
  17.3 15.7 %all_to_all.24 = f32[16,1,128]{2,1,0:T(1,128)S(1)} all-to-all(f32[16,1,128]{2,1,0:T(1,128)S(1)} %broadcast_in_dim.7), channel_id=1, replica_groups=mesh['rad'=16,'mode'=16] {'mode'}, dimensions={0} | all-to-all | bytes 16384 | tf_op jit(solution)/shard_map/all_to_all | solution.py:276
  33.0 0.0 collective-permute-done.2.cross_ref
  33.0 0.0 copy-start.3
  33.0 0.0 collective-permute-done.1.same_ref
  33.0 0.0 copy-start.4
  33.0 0.0 collective-permute-done.refs_0_
  33.0 1.6 collective-permute-start.5
  34.6 0.6 broadcast_in_dim.16
  35.2 4.2 %all-to-all-start.1 = ((f32[8,16,128]{2,1,0:T(8,128)}), f32[8,16,128]{2,1,0:T(8,128)S(1)}, u32[]{:S(2)}, u32[]{:S(2)}) async-start(f32[8,16,128]{2,1,0:T(8,128)} %broadcast_in_dim.16), calls=%async_computation.1 | async-start | bytes 131072 | tf_op jit(solution)/shard_map/all_to_all | solution.py:287
  39.5 0.6 pad_add_fusion.place_ref
  40.1 4.6 %all-to-all-done.1.degree_ref = f32[8,16,128]{2,1,0:T(8,128)S(1)} async-done(((f32[8,16,128]{2,1,0:T(8,128)}), f32[8,16,128]{2,1,0:T(8,128)S(1)}, u32[]{:S(2)}, u32[]{:S(2)}) %all-to-all-start.1) | async-done | bytes 65568 | tf_op jit(solution)/shard_map/all_to_all | solution.py:287
  44.7 0.0 copy-start.2
  44.7 0.0 collective-permute-done.4.other_forcing_ref
  44.7 0.0 collective-permute-done.3.other_ref
  44.7 0.0 copy-done.3
  44.7 0.0 copy-done.4
  44.7 0.6 copy-done.2
  45.3 6.9 %right_side.1 = bf16[64,2,2,40,128]{4,3,2,1,0:T(8,128)(2,1)} custom-call(s32[3]{0:T(128)} %pad_add_fusion.place_ref, f32[8,16,128]{2,1,0:T(8,128)} %copy-done.2, f32[2,1,16384]{2,1,0:T(1,128)} %copy-done.4, f32[2,1,16384]{2,1,0:T(1,128)} %copy-done.3, f32[2,40,16384]{2,1,0:T(8,128)} %own_ref.2, bf16[2,40,16384]{2,1,0:T(8,128)(2,1)} %own_forcing_ref.1, ...), custom_call_target="tpu_custom_call" | custom-call | tf_op jit(solution)/shard_map/right_side/pallas_call | solution.py:292
  52.2 0.0 copy-start
  52.2 0.0 collective-permute-done.5.refs_1_
  52.2 56.9 %all_to_all.25 = bf16[64,2,2,40,128]{4,3,2,1,0:T(8,128)(2,1)S(1)} all-to-all(bf16[64,2,2,40,128]{4,3,2,1,0:T(8,128)(2,1)} %right_side.1), channel_id=1, replica_groups={{0,1,2,3,8,9,10,11,32,33,34,35,40,41,42,43,64,65,66,67,72,73,74,75,96,9..., dimensions={0} | all-to-all | bytes 5242880 | tf_op jit(solution)/shard_map/all_to_all | solution.py:310
  109.1 0.0 copy-done
  109.1 3.2 %solve.1 = bf16[8,8,2,2,40,128]{5,4,3,2,1,0:T(8,128)(2,1)S(1)} custom-call(bf16[2,1,640,640]{3,2,1,0:T(8,128)(2,1)S(1)} %copy-done, bf16[2,1,320,640]{3,2,1,0:T(8,128)(2,1)S(1)} %collective-permute-done.refs_0_, bf16[2,1,320,640]{3,2,1,0:T(8,128)(2,1)S(1)} %collective-permute-done.5.refs_1_, bf16[8,8,2,2,40,128]{5,4,3,2,1,0:T(8,128)(2,1)S(1)} %bitcast.7), custom_call_target="tpu_custom_call" | custom-call | tf_op jit(solution)/shard_map/solve/pallas_call | solution.py:320
  112.3 0.0 copy-start.1
  112.3 55.2 %all_to_all.26.solved_ref = bf16[64,2,2,40,128]{4,3,2,1,0:T(8,128)(2,1)S(1)} all-to-all(bf16[64,2,2,40,128]{4,3,2,1,0:T(8,128)(2,1)S(1)} %bitcast.8), channel_id=1, replica_groups={{0,1,2,3,8,9,10,11,32,33,34,35,40,41,42,43,64,65,66,67,72,73,74,75,96,9..., dimensions={0} | all-to-all | bytes 5242880 | tf_op jit(solution)/shard_map/all_to_all | solution.py:330
  167.6 0.0 collective-permute-start.6
  167.6 0.0 copy-done.1
  167.6 3.0 %unpack_own.1.refs_0_ = bf16[2,40,16384]{2,1,0:T(8,128)(2,1)} custom-call(s32[3]{0:T(128)S(1)} %copy-done.1, bf16[64,2,2,40,128]{4,3,2,1,0:T(8,128)(2,1)S(1)} %all_to_all.26.solved_ref), custom_call_target="tpu_custom_call" | custom-call | flops 2621440 | bytes 2621440 | tf_op jit(solution)/shard_map/unpack_own/pallas_call | solution.py:340
  170.6 1.9 %collective-permute-done.6.solved_ref = bf16[64,2,2,40,128]{4,3,2,1,0:T(8,128)(2,1)S(1)} collective-permute-done((bf16[64,2,2,40,128]{4,3,2,1,0:T(8,128)(2,1)S(1)}, bf16[64,2,2,40,128]{4,3,2,1,0:T(8,128)(2,1)S(1)}, u32[]{:S(2)}, u32[]{:S(2)}) %collective-permute-start.6) | collective-permute-done | bytes 2621472 | tf_op jit(solution)/shard_map/ppermute | solution.py:359
  172.5 3.0 %unpack_other.1 = bf16[2,40,16384]{2,1,0:T(8,128)(2,1)} custom-call(s32[3]{0:T(128)S(1)} %copy-done.1, bf16[64,2,2,40,128]{4,3,2,1,0:T(8,128)(2,1)S(1)} %collective-permute-done.6.solved_ref, bf16[2,40,16384]{2,1,0:T(8,128)(2,1)} %unpack_own.1.refs_0_), custom_call_target="tpu_custom_call", output_to_operand_aliasing={{}: (2, {})} | custom-call | flops 2621440 | bytes 2621440 | tf_op jit(solution)/shard_map/unpack_other/pallas_call | solution.py:340
  (1 shorter events, 0.0 us)
Async XLA Ops:
  0.0 44.7 %collective-permute-start.3 = (f32[2,40,16384]{2,1,0:T(8,128)}, f32[2,40,16384]{2,1,0:T(8,128)}, u32[]{:S(2)}, u32[]{:S(2)}) collective-permute-start(f32[2,40,16384]{2,1,0:T(8,128)} %own_ref.2), channel_id=1, source_target_pairs={{0,16},{16,0},{32,48},{48,32},{64,80},{80,64},{96,112},{112,96},{1... | collective-permute-start | bytes 15728648 | tf_op jit(solution)/shard_map/ppermute | solution.py:274
  4.8 28.2 %collective-permute-start = (bf16[2,1,320,640]{3,2,1,0:T(8,128)(2,1)S(1)}, bf16[2,1,320,640]{3,2,1,0:T(8,128)(2,1)S(1)}, u32[]{:S(2)}, u32[]{:S(2)}) collective-permute-start(bf16[2,1,320,640]{3,2,1,0:T(8,128)(2,1)S(1)} %get-tuple-element.22), channel_id=1, source_target_pairs={{0,7},{1,6},{2,5},{3,4},{4,3},{5,2},{6,1},{7,0},{8,15},{9,14},{10,... | collective-permute-start | bytes 2457608 | tf_op jit(solution)/shard_map/ppermute | solution.py:277
  7.5 37.2 %collective-permute-start.4 = (bf16[2,40,16384]{2,1,0:T(8,128)(2,1)}, bf16[2,40,16384]{2,1,0:T(8,128)(2,1)}, u32[]{:S(2)}, u32[]{:S(2)}) collective-permute-start(bf16[2,40,16384]{2,1,0:T(8,128)(2,1)} %own_forcing_ref.1), channel_id=1, source_target_pairs={{0,16},{16,0},{32,48},{48,32},{64,80},{80,64},{96,112},{112,96},{1... | collective-permute-start | bytes 7864328 | tf_op jit(solution)/shard_map/ppermute | solution.py:273
  10.3 22.7 %collective-permute-start.2 = (f32[2,1,16384]{2,1,0:T(1,128)S(1)}, f32[2,1,16384]{2,1,0:T(1,128)S(1)}, u32[]{:S(2)}, u32[]{:S(2)}) collective-permute-start(f32[2,1,16384]{2,1,0:T(1,128)S(1)} %constant_dynamic-slice_fusion), channel_id=1, source_target_pairs={{16,32},{48,64},{80,96},{112,128},{144,160},{176,192},{208,224},{3... | collective-permute-start | bytes 393224 | tf_op jit(solution)/shard_map/ppermute | solution.py:280
  13.4 19.6 %collective-permute-start.1 = (f32[2,1,16384]{2,1,0:T(1,128)S(1)}, f32[2,1,16384]{2,1,0:T(1,128)S(1)}, u32[]{:S(2)}, u32[]{:S(2)}) collective-permute-start(f32[2,1,16384]{2,1,0:T(1,128)S(1)} %constant_dynamic-slice_fusion), channel_id=1, source_target_pairs={{16,48},{48,80},{80,112},{112,144},{144,176},{176,208},{208,240},{... | collective-permute-start | bytes 393224 | tf_op jit(solution)/shard_map/ppermute | solution.py:279
  33.0 11.7 %copy-start.3 = (f32[2,1,16384]{2,1,0:T(1,128)}, f32[2,1,16384]{2,1,0:T(1,128)S(1)}, u32[]{:S(2)}) copy-start(f32[2,1,16384]{2,1,0:T(1,128)S(1)} %collective-permute-done.2.cross_ref) | copy-start | bytes 393220
  33.0 11.7 %copy-start.4 = (f32[2,1,16384]{2,1,0:T(1,128)}, f32[2,1,16384]{2,1,0:T(1,128)S(1)}, u32[]{:S(2)}) copy-start(f32[2,1,16384]{2,1,0:T(1,128)S(1)} %collective-permute-done.1.same_ref) | copy-start | bytes 393220
  33.0 19.2 %collective-permute-start.5 = (bf16[2,1,320,640]{3,2,1,0:T(8,128)(2,1)S(1)}, bf16[2,1,320,640]{3,2,1,0:T(8,128)(2,1)S(1)}, u32[]{:S(2)}, u32[]{:S(2)}) collective-permute-start(bf16[2,1,320,640]{3,2,1,0:T(8,128)(2,1)S(1)} %get-tuple-element.18), channel_id=1, source_target_pairs={{0,7},{1,6},{2,5},{3,4},{4,3},{5,2},{6,1},{7,0},{8,15},{9,14},{10,... | collective-permute-start | bytes 2457608 | tf_op jit(solution)/shard_map/ppermute | solution.py:285
  35.2 9.4 %all-to-all-start.1 = ((f32[8,16,128]{2,1,0:T(8,128)}), f32[8,16,128]{2,1,0:T(8,128)S(1)}, u32[]{:S(2)}, u32[]{:S(2)}) async-start(f32[8,16,128]{2,1,0:T(8,128)} %broadcast_in_dim.16), calls=%async_computation.1 | async-start | bytes 131072 | tf_op jit(solution)/shard_map/all_to_all | solution.py:287
  44.7 0.6 copy-start.2
  52.2 56.9 %copy-start = (bf16[2,1,640,640]{3,2,1,0:T(8,128)(2,1)S(1)}, bf16[2,1,640,640]{3,2,1,0:T(8,128)(2,1)}, u32[]{:S(2)}) copy-start(bf16[2,1,640,640]{3,2,1,0:T(8,128)(2,1)} %own_ref.3) | copy-start | bytes 4915204
  112.3 55.2 %copy-start.1 = (s32[3]{0:T(128)S(1)}, s32[3]{0:T(128)}, u32[]{:S(2)}) copy-start(s32[3]{0:T(128)} %pad_add_fusion.place_ref) | copy-start | bytes 40
  167.6 4.9 %collective-permute-start.6 = (bf16[64,2,2,40,128]{4,3,2,1,0:T(8,128)(2,1)S(1)}, bf16[64,2,2,40,128]{4,3,2,1,0:T(8,128)(2,1)S(1)}, u32[]{:S(2)}, u32[]{:S(2)}) collective-permute-start(bf16[64,2,2,40,128]{4,3,2,1,0:T(8,128)(2,1)S(1)} %all_to_all.26.solved_ref), channel_id=1, source_target_pairs={{0,16},{16,0},{32,48},{48,32},{64,80},{80,64},{96,112},{112,96},{1... | collective-permute-start | bytes 7864328 | tf_op jit(solution)/shard_map/ppermute | solution.py:359
